TPU v7x, 1024 devices: a whole 8x8x8 slice. The times are simulated.
1024 devices in a mesh: rad: 16 (over z, core), lat: 8 (over x), lon: 8 (over y).
Axes of the slice: x: 8, y: 8, z: 8, core: 2. Of those that a mesh axis runs over, the one named last changes fastest.
Arguments:
- gradient: float32 [64, 128, 1024], P('rad', 'lat', 'lon')
- conductance: float32 [64, 128, 1024], P('rad', 'lat', 'lon'), may hold values from 0.3 to 1
- s_hist: float32 [10, 64, 128, 1024], P(None, 'rad', 'lat', 'lon')
- y_hist: float32 [10, 64, 128, 1024], P(None, 'rad', 'lat', 'lon'), as said below
Outputs:
- smoothed: float32 [64, 128, 1024], P('rad', 'lat', 'lon')
- direction: float32 [64, 128, 1024], P('rad', 'lat', 'lon')
Inputs may be any that keep to these rules, and one draw needn't show every extreme that they name: For every pair the sum over all cells of s_hist times y_hist is positive.
All inputs are finite; a program needn't handle non-finite values.
Results may differ from a plain program's by a relative error of at most 0.00021.
Values sent between devices are 32-bit elements; how exact they have to be, the bound alone decides.
A program may use at most 32 MiB of HBM per device.

v0:
```python
import jax
import jax.numpy as jnp
from jax import lax
from jax.sharding import PartitionSpec as P

STEPS = 12


radial_weight = 0.05
latitude_weight = 0.15
longitude_weight = 0.25


def padded(x, sides, width):
    for axis, dim in sides:
        peers, length = (lax.axis_size(axis), x.shape[dim])
        up = [(i, (i + 1) % peers) for i in range(peers)]
        down = [(j, i) for i, j in up]
        last = lax.slice_in_dim(x, length - width, length, axis=dim)
        first = lax.slice_in_dim(x, 0, width, axis=dim)
        before = lax.ppermute(last, axis, up)
        after = lax.ppermute(first, axis, down)
        x = jnp.concatenate([before, x, after], axis=dim)
    return x


def relax(box, kappa):
    center = box[1:-1, 1:-1, 1:-1]
    lap_r = box[2:, 1:-1, 1:-1] + box[:-2, 1:-1, 1:-1] - 2.0 * center
    lap_a = box[1:-1, 2:, 1:-1] + box[1:-1, :-2, 1:-1] - 2.0 * center
    lap_o = box[1:-1, 1:-1, 2:] + box[1:-1, 1:-1, :-2] - 2.0 * center
    return center + kappa * (
        radial_weight * lap_r + latitude_weight * lap_a + longitude_weight * lap_o
    )


def inside_mask(width, rad_dev, lat_dev):
    rad_pos = lax.axis_index("rad") * rad_dev + jnp.arange(-width, rad_dev + width, dtype=jnp.int32)
    lat_pos = lax.axis_index("lat") * lat_dev + jnp.arange(-width, lat_dev + width, dtype=jnp.int32)
    rad_inside = (rad_pos >= 0) & (rad_pos < rad_dev * lax.axis_size("rad"))
    lat_inside = (lat_pos >= 0) & (lat_pos < lat_dev * lax.axis_size("lat"))
    return (rad_inside[:, None, None] & lat_inside[None, :, None]).astype(jnp.float32)


def coefficients(pair_sy, pair_yy, pair_sg, pair_yg):
    count = pair_sy.shape[0]
    inverses = [1.0 / pair_sy[position, position] for position in range(count)]
    alphas = [None] * count
    for position in reversed(range(count)):
        total = pair_sg[position]
        for later in range(position + 1, count):
            total = total - alphas[later] * pair_sy[position, later]
        alphas[position] = inverses[position] * total
    scaling = pair_sy[count - 1, count - 1] / pair_yy[count - 1, count - 1]
    step_weights = []
    for position in range(count):
        total = scaling * pair_yg[position]
        for other in range(count):
            total = total - scaling * alphas[other] * pair_yy[position, other]
        for earlier in range(position):
            total = total + step_weights[earlier] * pair_sy[earlier, position]
        step_weights.append(alphas[position] - inverses[position] * total)
    return (scaling, jnp.stack(alphas), jnp.stack(step_weights))


def per_device(gradient, conductance, s_hist, y_hist):
    rad_dev, lat_dev, lon_dev = gradient.shape
    count = s_hist.shape[0]
    highest = lax.Precision.HIGHEST
    flat_s = s_hist.reshape(count, -1)
    flat_y = y_hist.reshape(count, -1)
    mask_one = inside_mask(1, rad_dev, lat_dev)

    def one_pass(number, field):
        box = padded(field, (("rad", 0), ("lat", 1), ("lon", 2)), 1) * mask_one
        return relax(box, conductance)

    smoothed = lax.fori_loop(0, STEPS, one_pass, gradient)
    flat_g = smoothed.reshape(-1)
    local_sg = jnp.dot(flat_s, flat_g, precision=highest, preferred_element_type=jnp.float32)
    local_yg = jnp.dot(flat_y, flat_g, precision=highest, preferred_element_type=jnp.float32)
    pair_sy, pair_yy, pair_sg, pair_yg = lax.psum(
        (
            jnp.dot(flat_s, flat_y.T, precision=highest, preferred_element_type=jnp.float32),
            jnp.dot(flat_y, flat_y.T, precision=highest, preferred_element_type=jnp.float32),
            local_sg,
            local_yg,
        ),
        ("rad", "lat", "lon"),
    )
    scaling, alphas, step_weights = coefficients(pair_sy, pair_yy, pair_sg, pair_yg)
    along_y = jnp.einsum("p,pabc->abc", alphas, y_hist, precision=highest)
    along_s = jnp.einsum("p,pabc->abc", step_weights, s_hist, precision=highest)
    combined = scaling * smoothed - scaling * along_y + along_s
    return (smoothed, -combined)


def solution(mesh):
    placed = (
        P("rad", "lat", "lon"),
        P("rad", "lat", "lon"),
        P(None, "rad", "lat", "lon"),
        P(None, "rad", "lat", "lon"),
    )
    return jax.shard_map(
        per_device,
        mesh=mesh,
        in_specs=placed,
        out_specs=(P("rad", "lat", "lon"), P("rad", "lat", "lon")),
        check_vma=False,
    )
```

profile of v0, /device:TPU:1, one launch (start us, length us, event | category | flops | bytes accessed | tf_op | source)
XLA Modules:
  0.0 561.9 jit_solution(1797507231923193649)
XLA Ops:
  1.4 292.5 %while.11 = (s32[]{:T(128)}, f32[4,16,128]{2,1,0:T(8,128)S(1)}, f32[4,16,128]{2,1,0:T(8,128)S(1)}, pred[18]{0:T(512)(128)(4,1)S(1)}, pred[6]{0:T(512)(128)(4,1)S(1)}, /*index=5*/s32[]{:T(128)}) while((s32[]{:T(128)}, f32[4,16,128]{2,1,0:T(8,128)S(1)}, f32[4,16,128]{2,1,0:T(8,128)S(1)}, pred[18]{0:T(512)(128)(4,1)S(1)}, ...), condition=%wide.region_1.0_spmd.clone, body=%wide.region_0.0_spmd.clone.sunk | while | flops 212754 | bytes 757677 | solution.py:78
  1.4 4.4 collective-permute-start
  5.8 9.8 %collective-permute-start.1 = (f32[1,16,128]{2,1,0:T(8,128)S(1)}, f32[1,16,128]{2,1,0:T(8,128)S(1)}, u32[]{:S(2)}, u32[]{:S(2)}) collective-permute-start(f32[1,16,128]{2,1,0:T(8,128)S(1)} %get-tuple-element.272), channel_id=1, source_target_pairs={{64,0},{128,64},{192,128},{256,192},{320,256},{384,320},{448,384},... | collective-permute-start | bytes 24584 | tf_op jit(solution)/shard_map/while/body/eval_jaxpr/ppermute | solution.py:22
  18.3 3.4 collective-permute-start.3
  25.9 3.4 collective-permute-start.5
  29.4 2.9 collective-permute-done.5
  32.6 3.4 collective-permute-start
  36.0 8.8 %collective-permute-start.1 = (f32[1,16,128]{2,1,0:T(8,128)S(1)}, f32[1,16,128]{2,1,0:T(8,128)S(1)}, u32[]{:S(2)}, u32[]{:S(2)}) collective-permute-start(f32[1,16,128]{2,1,0:T(8,128)S(1)} %get-tuple-element.272), channel_id=1, source_target_pairs={{64,0},{128,64},{192,128},{256,192},{320,256},{384,320},{448,384},... | collective-permute-start | bytes 24584 | tf_op jit(solution)/shard_map/while/body/eval_jaxpr/ppermute | solution.py:22
  47.5 3.4 collective-permute-start.3
  55.1 3.4 collective-permute-start.5
  58.5 2.9 collective-permute-done.5
  61.8 6.0 %collective-permute-start.1 = (f32[1,16,128]{2,1,0:T(8,128)S(1)}, f32[1,16,128]{2,1,0:T(8,128)S(1)}, u32[]{:S(2)}, u32[]{:S(2)}) collective-permute-start(f32[1,16,128]{2,1,0:T(8,128)S(1)} %get-tuple-element.272), channel_id=1, source_target_pairs={{64,0},{128,64},{192,128},{256,192},{320,256},{384,320},{448,384},... | collective-permute-start | bytes 24584 | tf_op jit(solution)/shard_map/while/body/eval_jaxpr/ppermute | solution.py:22
  70.5 3.4 collective-permute-start.3
  78.1 3.4 collective-permute-start.5
  81.6 2.9 collective-permute-done.5
  84.8 6.0 %collective-permute-start.1 = (f32[1,16,128]{2,1,0:T(8,128)S(1)}, f32[1,16,128]{2,1,0:T(8,128)S(1)}, u32[]{:S(2)}, u32[]{:S(2)}) collective-permute-start(f32[1,16,128]{2,1,0:T(8,128)S(1)} %get-tuple-element.272), channel_id=1, source_target_pairs={{64,0},{128,64},{192,128},{256,192},{320,256},{384,320},{448,384},... | collective-permute-start | bytes 24584 | tf_op jit(solution)/shard_map/while/body/eval_jaxpr/ppermute | solution.py:22
  93.5 3.4 collective-permute-start.3
  101.1 3.4 collective-permute-start.5
  104.6 2.9 collective-permute-done.5
  107.8 6.0 %collective-permute-start.1 = (f32[1,16,128]{2,1,0:T(8,128)S(1)}, f32[1,16,128]{2,1,0:T(8,128)S(1)}, u32[]{:S(2)}, u32[]{:S(2)}) collective-permute-start(f32[1,16,128]{2,1,0:T(8,128)S(1)} %get-tuple-element.272), channel_id=1, source_target_pairs={{64,0},{128,64},{192,128},{256,192},{320,256},{384,320},{448,384},... | collective-permute-start | bytes 24584 | tf_op jit(solution)/shard_map/while/body/eval_jaxpr/ppermute | solution.py:22
  116.8 3.1 collective-permute-start.3
  124.4 3.3 collective-permute-start.5
  127.8 2.9 collective-permute-done.5
  131.1 6.3 %collective-permute-start.1 = (f32[1,16,128]{2,1,0:T(8,128)S(1)}, f32[1,16,128]{2,1,0:T(8,128)S(1)}, u32[]{:S(2)}, u32[]{:S(2)}) collective-permute-start(f32[1,16,128]{2,1,0:T(8,128)S(1)} %get-tuple-element.272), channel_id=1, source_target_pairs={{64,0},{128,64},{192,128},{256,192},{320,256},{384,320},{448,384},... | collective-permute-start | bytes 24584 | tf_op jit(solution)/shard_map/while/body/eval_jaxpr/ppermute | solution.py:22
  140.2 3.4 collective-permute-start.3
  147.8 3.4 collective-permute-start.5
  151.2 2.9 collective-permute-done.5
  154.4 5.8 %collective-permute-start.1 = (f32[1,16,128]{2,1,0:T(8,128)S(1)}, f32[1,16,128]{2,1,0:T(8,128)S(1)}, u32[]{:S(2)}, u32[]{:S(2)}) collective-permute-start(f32[1,16,128]{2,1,0:T(8,128)S(1)} %get-tuple-element.272), channel_id=1, source_target_pairs={{64,0},{128,64},{192,128},{256,192},{320,256},{384,320},{448,384},... | collective-permute-start | bytes 24584 | tf_op jit(solution)/shard_map/while/body/eval_jaxpr/ppermute | solution.py:22
  163.0 3.4 collective-permute-start.3
  170.6 3.4 collective-permute-start.5
  174.0 2.9 collective-permute-done.5
  177.2 5.8 %collective-permute-start.1 = (f32[1,16,128]{2,1,0:T(8,128)S(1)}, f32[1,16,128]{2,1,0:T(8,128)S(1)}, u32[]{:S(2)}, u32[]{:S(2)}) collective-permute-start(f32[1,16,128]{2,1,0:T(8,128)S(1)} %get-tuple-element.272), channel_id=1, source_target_pairs={{64,0},{128,64},{192,128},{256,192},{320,256},{384,320},{448,384},... | collective-permute-start | bytes 24584 | tf_op jit(solution)/shard_map/while/body/eval_jaxpr/ppermute | solution.py:22
  185.8 3.4 collective-permute-start.3
  196.8 3.4 collective-permute-done.5
  200.5 6.1 %collective-permute-start.1 = (f32[1,16,128]{2,1,0:T(8,128)S(1)}, f32[1,16,128]{2,1,0:T(8,128)S(1)}, u32[]{:S(2)}, u32[]{:S(2)}) collective-permute-start(f32[1,16,128]{2,1,0:T(8,128)S(1)} %get-tuple-element.272), channel_id=1, source_target_pairs={{64,0},{128,64},{192,128},{256,192},{320,256},{384,320},{448,384},... | collective-permute-start | bytes 24584 | tf_op jit(solution)/shard_map/while/body/eval_jaxpr/ppermute | solution.py:22
  220.9 3.4 collective-permute-done.5
  224.6 6.3 %collective-permute-start.1 = (f32[1,16,128]{2,1,0:T(8,128)S(1)}, f32[1,16,128]{2,1,0:T(8,128)S(1)}, u32[]{:S(2)}, u32[]{:S(2)}) collective-permute-start(f32[1,16,128]{2,1,0:T(8,128)S(1)} %get-tuple-element.272), channel_id=1, source_target_pairs={{64,0},{128,64},{192,128},{256,192},{320,256},{384,320},{448,384},... | collective-permute-start | bytes 24584 | tf_op jit(solution)/shard_map/while/body/eval_jaxpr/ppermute | solution.py:22
  233.7 3.4 collective-permute-start.3
  241.3 3.4 collective-permute-start.5
  244.8 2.9 collective-permute-done.5
  248.0 6.0 %collective-permute-start.1 = (f32[1,16,128]{2,1,0:T(8,128)S(1)}, f32[1,16,128]{2,1,0:T(8,128)S(1)}, u32[]{:S(2)}, u32[]{:S(2)}) collective-permute-start(f32[1,16,128]{2,1,0:T(8,128)S(1)} %get-tuple-element.272), channel_id=1, source_target_pairs={{64,0},{128,64},{192,128},{256,192},{320,256},{384,320},{448,384},... | collective-permute-start | bytes 24584 | tf_op jit(solution)/shard_map/while/body/eval_jaxpr/ppermute | solution.py:22
  256.7 3.4 collective-permute-start.3
  264.3 3.4 collective-permute-start.5
  271.0 6.0 %collective-permute-start.1 = (f32[1,16,128]{2,1,0:T(8,128)S(1)}, f32[1,16,128]{2,1,0:T(8,128)S(1)}, u32[]{:S(2)}, u32[]{:S(2)}) collective-permute-start(f32[1,16,128]{2,1,0:T(8,128)S(1)} %get-tuple-element.272), channel_id=1, source_target_pairs={{64,0},{128,64},{192,128},{256,192},{320,256},{384,320},{448,384},... | collective-permute-start | bytes 24584 | tf_op jit(solution)/shard_map/while/body/eval_jaxpr/ppermute | solution.py:22
  279.8 3.4 collective-permute-start.3
  287.3 3.4 collective-permute-start.5
  290.8 2.9 collective-permute-done.5
  297.6 115.2 %all-reduce = (f32[10,10]{1,0:T(8,128)S(1)}, f32[10]{0:T(128)S(1)}, f32[10,10]{1,0:T(8,128)S(1)}, f32[10]{0:T(128)S(1)}) all-reduce(f32[10,10]{1,0:T(8,128)S(1)} %convolution_bitcast_fusion.1, f32[10]{0:T(128)S(1)} %convolution_bitcast_fusion.3, ...), channel_id=1, replica_groups=mesh['rad'=16,'lat'=8,'lon'=8] {'rad','lat','lon'}, use_global_device_ids=true, to_apply=%region_2.0 | all-reduce | flops 220 | bytes 1760 | tf_op jit(solution)/shard_map/psum | solution.py:82
  (250 shorter events, 116.1 us)
Async XLA Ops:
  1.4 14.8 %collective-permute-start = (f32[1,16,128]{2,1,0:T(8,128)S(1)}, f32[1,16,128]{2,1,0:T(8,128)S(1)}, u32[]{:S(2)}, u32[]{:S(2)}) collective-permute-start(f32[1,16,128]{2,1,0:T(8,128)S(1)} %get-tuple-element.271), channel_id=1, source_target_pairs={{0,64},{64,128},{128,192},{192,256},{256,320},{320,384},{384,448},... | collective-permute-start | bytes 24584 | tf_op jit(solution)/shard_map/while/body/eval_jaxpr/ppermute | solution.py:21
  5.8 10.6 %collective-permute-start.1 = (f32[1,16,128]{2,1,0:T(8,128)S(1)}, f32[1,16,128]{2,1,0:T(8,128)S(1)}, u32[]{:S(2)}, u32[]{:S(2)}) collective-permute-start(f32[1,16,128]{2,1,0:T(8,128)S(1)} %get-tuple-element.272), channel_id=1, source_target_pairs={{64,0},{128,64},{192,128},{256,192},{320,256},{384,320},{448,384},... | collective-permute-start | bytes 24584 | tf_op jit(solution)/shard_map/while/body/eval_jaxpr/ppermute | solution.py:22
  18.3 5.6 collective-permute-start.3
  25.9 6.3 %collective-permute-start.5 = (f32[6,18,1]{2,1,0:T(8,128)S(1)}, f32[6,18,1]{2,1,0:T(8,128)S(1)}, u32[]{:S(2)}, u32[]{:S(2)}) collective-permute-start(f32[6,18,1]{2,1,0:T(8,128)S(1)} %get-tuple-element.276), channel_id=1, source_target_pairs={{0,1},{1,2},{2,3},{3,4},{4,5},{5,6},{6,7},{7,0},{8,9},{9,10},{10,1... | collective-permute-start | bytes 1304 | tf_op jit(solution)/shard_map/while/body/eval_jaxpr/ppermute | solution.py:21
  32.6 12.8 %collective-permute-start = (f32[1,16,128]{2,1,0:T(8,128)S(1)}, f32[1,16,128]{2,1,0:T(8,128)S(1)}, u32[]{:S(2)}, u32[]{:S(2)}) collective-permute-start(f32[1,16,128]{2,1,0:T(8,128)S(1)} %get-tuple-element.271), channel_id=1, source_target_pairs={{0,64},{64,128},{128,192},{192,256},{256,320},{320,384},{384,448},... | collective-permute-start | bytes 24584 | tf_op jit(solution)/shard_map/while/body/eval_jaxpr/ppermute | solution.py:21
  36.0 9.6 %collective-permute-start.1 = (f32[1,16,128]{2,1,0:T(8,128)S(1)}, f32[1,16,128]{2,1,0:T(8,128)S(1)}, u32[]{:S(2)}, u32[]{:S(2)}) collective-permute-start(f32[1,16,128]{2,1,0:T(8,128)S(1)} %get-tuple-element.272), channel_id=1, source_target_pairs={{64,0},{128,64},{192,128},{256,192},{320,256},{384,320},{448,384},... | collective-permute-start | bytes 24584 | tf_op jit(solution)/shard_map/while/body/eval_jaxpr/ppermute | solution.py:22
  47.5 5.6 collective-permute-start.3
  55.1 6.3 %collective-permute-start.5 = (f32[6,18,1]{2,1,0:T(8,128)S(1)}, f32[6,18,1]{2,1,0:T(8,128)S(1)}, u32[]{:S(2)}, u32[]{:S(2)}) collective-permute-start(f32[6,18,1]{2,1,0:T(8,128)S(1)} %get-tuple-element.276), channel_id=1, source_target_pairs={{0,1},{1,2},{2,3},{3,4},{4,5},{5,6},{6,7},{7,0},{8,9},{9,10},{10,1... | collective-permute-start | bytes 1304 | tf_op jit(solution)/shard_map/while/body/eval_jaxpr/ppermute | solution.py:21
  61.7 6.7 %collective-permute-start = (f32[1,16,128]{2,1,0:T(8,128)S(1)}, f32[1,16,128]{2,1,0:T(8,128)S(1)}, u32[]{:S(2)}, u32[]{:S(2)}) collective-permute-start(f32[1,16,128]{2,1,0:T(8,128)S(1)} %get-tuple-element.271), channel_id=1, source_target_pairs={{0,64},{64,128},{128,192},{192,256},{256,320},{320,384},{384,448},... | collective-permute-start | bytes 24584 | tf_op jit(solution)/shard_map/while/body/eval_jaxpr/ppermute | solution.py:21
  61.8 6.8 %collective-permute-start.1 = (f32[1,16,128]{2,1,0:T(8,128)S(1)}, f32[1,16,128]{2,1,0:T(8,128)S(1)}, u32[]{:S(2)}, u32[]{:S(2)}) collective-permute-start(f32[1,16,128]{2,1,0:T(8,128)S(1)} %get-tuple-element.272), channel_id=1, source_target_pairs={{64,0},{128,64},{192,128},{256,192},{320,256},{384,320},{448,384},... | collective-permute-start | bytes 24584 | tf_op jit(solution)/shard_map/while/body/eval_jaxpr/ppermute | solution.py:22
  70.5 5.6 collective-permute-start.3
  78.1 6.3 %collective-permute-start.5 = (f32[6,18,1]{2,1,0:T(8,128)S(1)}, f32[6,18,1]{2,1,0:T(8,128)S(1)}, u32[]{:S(2)}, u32[]{:S(2)}) collective-permute-start(f32[6,18,1]{2,1,0:T(8,128)S(1)} %get-tuple-element.276), channel_id=1, source_target_pairs={{0,1},{1,2},{2,3},{3,4},{4,5},{5,6},{6,7},{7,0},{8,9},{9,10},{10,1... | collective-permute-start | bytes 1304 | tf_op jit(solution)/shard_map/while/body/eval_jaxpr/ppermute | solution.py:21
  84.7 6.7 %collective-permute-start = (f32[1,16,128]{2,1,0:T(8,128)S(1)}, f32[1,16,128]{2,1,0:T(8,128)S(1)}, u32[]{:S(2)}, u32[]{:S(2)}) collective-permute-start(f32[1,16,128]{2,1,0:T(8,128)S(1)} %get-tuple-element.271), channel_id=1, source_target_pairs={{0,64},{64,128},{128,192},{192,256},{256,320},{320,384},{384,448},... | collective-permute-start | bytes 24584 | tf_op jit(solution)/shard_map/while/body/eval_jaxpr/ppermute | solution.py:21
  84.8 6.8 %collective-permute-start.1 = (f32[1,16,128]{2,1,0:T(8,128)S(1)}, f32[1,16,128]{2,1,0:T(8,128)S(1)}, u32[]{:S(2)}, u32[]{:S(2)}) collective-permute-start(f32[1,16,128]{2,1,0:T(8,128)S(1)} %get-tuple-element.272), channel_id=1, source_target_pairs={{64,0},{128,64},{192,128},{256,192},{320,256},{384,320},{448,384},... | collective-permute-start | bytes 24584 | tf_op jit(solution)/shard_map/while/body/eval_jaxpr/ppermute | solution.py:22
  93.5 5.6 collective-permute-start.3
  101.1 6.3 %collective-permute-start.5 = (f32[6,18,1]{2,1,0:T(8,128)S(1)}, f32[6,18,1]{2,1,0:T(8,128)S(1)}, u32[]{:S(2)}, u32[]{:S(2)}) collective-permute-start(f32[6,18,1]{2,1,0:T(8,128)S(1)} %get-tuple-element.276), channel_id=1, source_target_pairs={{0,1},{1,2},{2,3},{3,4},{4,5},{5,6},{6,7},{7,0},{8,9},{9,10},{10,1... | collective-permute-start | bytes 1304 | tf_op jit(solution)/shard_map/while/body/eval_jaxpr/ppermute | solution.py:21
  107.8 6.7 %collective-permute-start = (f32[1,16,128]{2,1,0:T(8,128)S(1)}, f32[1,16,128]{2,1,0:T(8,128)S(1)}, u32[]{:S(2)}, u32[]{:S(2)}) collective-permute-start(f32[1,16,128]{2,1,0:T(8,128)S(1)} %get-tuple-element.271), channel_id=1, source_target_pairs={{0,64},{64,128},{128,192},{192,256},{256,320},{320,384},{384,448},... | collective-permute-start | bytes 24584 | tf_op jit(solution)/shard_map/while/body/eval_jaxpr/ppermute | solution.py:21
  107.8 6.8 %collective-permute-start.1 = (f32[1,16,128]{2,1,0:T(8,128)S(1)}, f32[1,16,128]{2,1,0:T(8,128)S(1)}, u32[]{:S(2)}, u32[]{:S(2)}) collective-permute-start(f32[1,16,128]{2,1,0:T(8,128)S(1)} %get-tuple-element.272), channel_id=1, source_target_pairs={{64,0},{128,64},{192,128},{256,192},{320,256},{384,320},{448,384},... | collective-permute-start | bytes 24584 | tf_op jit(solution)/shard_map/while/body/eval_jaxpr/ppermute | solution.py:22
  116.8 5.6 collective-permute-start.3
  124.4 6.3 %collective-permute-start.5 = (f32[6,18,1]{2,1,0:T(8,128)S(1)}, f32[6,18,1]{2,1,0:T(8,128)S(1)}, u32[]{:S(2)}, u32[]{:S(2)}) collective-permute-start(f32[6,18,1]{2,1,0:T(8,128)S(1)} %get-tuple-element.276), channel_id=1, source_target_pairs={{0,1},{1,2},{2,3},{3,4},{4,5},{5,6},{6,7},{7,0},{8,9},{9,10},{10,1... | collective-permute-start | bytes 1304 | tf_op jit(solution)/shard_map/while/body/eval_jaxpr/ppermute | solution.py:21
  131.1 7.0 %collective-permute-start = (f32[1,16,128]{2,1,0:T(8,128)S(1)}, f32[1,16,128]{2,1,0:T(8,128)S(1)}, u32[]{:S(2)}, u32[]{:S(2)}) collective-permute-start(f32[1,16,128]{2,1,0:T(8,128)S(1)} %get-tuple-element.271), channel_id=1, source_target_pairs={{0,64},{64,128},{128,192},{192,256},{256,320},{320,384},{384,448},... | collective-permute-start | bytes 24584 | tf_op jit(solution)/shard_map/while/body/eval_jaxpr/ppermute | solution.py:21
  131.1 7.2 %collective-permute-start.1 = (f32[1,16,128]{2,1,0:T(8,128)S(1)}, f32[1,16,128]{2,1,0:T(8,128)S(1)}, u32[]{:S(2)}, u32[]{:S(2)}) collective-permute-start(f32[1,16,128]{2,1,0:T(8,128)S(1)} %get-tuple-element.272), channel_id=1, source_target_pairs={{64,0},{128,64},{192,128},{256,192},{320,256},{384,320},{448,384},... | collective-permute-start | bytes 24584 | tf_op jit(solution)/shard_map/while/body/eval_jaxpr/ppermute | solution.py:22
  140.2 5.6 collective-permute-start.3
  147.8 6.3 %collective-permute-start.5 = (f32[6,18,1]{2,1,0:T(8,128)S(1)}, f32[6,18,1]{2,1,0:T(8,128)S(1)}, u32[]{:S(2)}, u32[]{:S(2)}) collective-permute-start(f32[6,18,1]{2,1,0:T(8,128)S(1)} %get-tuple-element.276), channel_id=1, source_target_pairs={{0,1},{1,2},{2,3},{3,4},{4,5},{5,6},{6,7},{7,0},{8,9},{9,10},{10,1... | collective-permute-start | bytes 1304 | tf_op jit(solution)/shard_map/while/body/eval_jaxpr/ppermute | solution.py:21
  154.4 6.4 %collective-permute-start = (f32[1,16,128]{2,1,0:T(8,128)S(1)}, f32[1,16,128]{2,1,0:T(8,128)S(1)}, u32[]{:S(2)}, u32[]{:S(2)}) collective-permute-start(f32[1,16,128]{2,1,0:T(8,128)S(1)} %get-tuple-element.271), channel_id=1, source_target_pairs={{0,64},{64,128},{128,192},{192,256},{256,320},{320,384},{384,448},... | collective-permute-start | bytes 24584 | tf_op jit(solution)/shard_map/while/body/eval_jaxpr/ppermute | solution.py:21
  154.4 6.6 %collective-permute-start.1 = (f32[1,16,128]{2,1,0:T(8,128)S(1)}, f32[1,16,128]{2,1,0:T(8,128)S(1)}, u32[]{:S(2)}, u32[]{:S(2)}) collective-permute-start(f32[1,16,128]{2,1,0:T(8,128)S(1)} %get-tuple-element.272), channel_id=1, source_target_pairs={{64,0},{128,64},{192,128},{256,192},{320,256},{384,320},{448,384},... | collective-permute-start | bytes 24584 | tf_op jit(solution)/shard_map/while/body/eval_jaxpr/ppermute | solution.py:22
  163.0 5.6 collective-permute-start.3
  170.6 6.3 %collective-permute-start.5 = (f32[6,18,1]{2,1,0:T(8,128)S(1)}, f32[6,18,1]{2,1,0:T(8,128)S(1)}, u32[]{:S(2)}, u32[]{:S(2)}) collective-permute-start(f32[6,18,1]{2,1,0:T(8,128)S(1)} %get-tuple-element.276), channel_id=1, source_target_pairs={{0,1},{1,2},{2,3},{3,4},{4,5},{5,6},{6,7},{7,0},{8,9},{9,10},{10,1... | collective-permute-start | bytes 1304 | tf_op jit(solution)/shard_map/while/body/eval_jaxpr/ppermute | solution.py:21
  177.2 6.5 %collective-permute-start = (f32[1,16,128]{2,1,0:T(8,128)S(1)}, f32[1,16,128]{2,1,0:T(8,128)S(1)}, u32[]{:S(2)}, u32[]{:S(2)}) collective-permute-start(f32[1,16,128]{2,1,0:T(8,128)S(1)} %get-tuple-element.271), channel_id=1, source_target_pairs={{0,64},{64,128},{128,192},{192,256},{256,320},{320,384},{384,448},... | collective-permute-start | bytes 24584 | tf_op jit(solution)/shard_map/while/body/eval_jaxpr/ppermute | solution.py:21
  177.2 6.6 %collective-permute-start.1 = (f32[1,16,128]{2,1,0:T(8,128)S(1)}, f32[1,16,128]{2,1,0:T(8,128)S(1)}, u32[]{:S(2)}, u32[]{:S(2)}) collective-permute-start(f32[1,16,128]{2,1,0:T(8,128)S(1)} %get-tuple-element.272), channel_id=1, source_target_pairs={{64,0},{128,64},{192,128},{256,192},{320,256},{384,320},{448,384},... | collective-permute-start | bytes 24584 | tf_op jit(solution)/shard_map/while/body/eval_jaxpr/ppermute | solution.py:22
  185.8 5.6 collective-permute-start.3
  193.9 6.3 %collective-permute-start.5 = (f32[6,18,1]{2,1,0:T(8,128)S(1)}, f32[6,18,1]{2,1,0:T(8,128)S(1)}, u32[]{:S(2)}, u32[]{:S(2)}) collective-permute-start(f32[6,18,1]{2,1,0:T(8,128)S(1)} %get-tuple-element.276), channel_id=1, source_target_pairs={{0,1},{1,2},{2,3},{3,4},{4,5},{5,6},{6,7},{7,0},{8,9},{9,10},{10,1... | collective-permute-start | bytes 1304 | tf_op jit(solution)/shard_map/while/body/eval_jaxpr/ppermute | solution.py:21
  200.5 6.7 %collective-permute-start = (f32[1,16,128]{2,1,0:T(8,128)S(1)}, f32[1,16,128]{2,1,0:T(8,128)S(1)}, u32[]{:S(2)}, u32[]{:S(2)}) collective-permute-start(f32[1,16,128]{2,1,0:T(8,128)S(1)} %get-tuple-element.271), channel_id=1, source_target_pairs={{0,64},{64,128},{128,192},{192,256},{256,320},{320,384},{384,448},... | collective-permute-start | bytes 24584 | tf_op jit(solution)/shard_map/while/body/eval_jaxpr/ppermute | solution.py:21
  200.5 6.9 %collective-permute-start.1 = (f32[1,16,128]{2,1,0:T(8,128)S(1)}, f32[1,16,128]{2,1,0:T(8,128)S(1)}, u32[]{:S(2)}, u32[]{:S(2)}) collective-permute-start(f32[1,16,128]{2,1,0:T(8,128)S(1)} %get-tuple-element.272), channel_id=1, source_target_pairs={{64,0},{128,64},{192,128},{256,192},{320,256},{384,320},{448,384},... | collective-permute-start | bytes 24584 | tf_op jit(solution)/shard_map/while/body/eval_jaxpr/ppermute | solution.py:22
  209.9 5.6 collective-permute-start.3
  218.0 6.3 %collective-permute-start.5 = (f32[6,18,1]{2,1,0:T(8,128)S(1)}, f32[6,18,1]{2,1,0:T(8,128)S(1)}, u32[]{:S(2)}, u32[]{:S(2)}) collective-permute-start(f32[6,18,1]{2,1,0:T(8,128)S(1)} %get-tuple-element.276), channel_id=1, source_target_pairs={{0,1},{1,2},{2,3},{3,4},{4,5},{5,6},{6,7},{7,0},{8,9},{9,10},{10,1... | collective-permute-start | bytes 1304 | tf_op jit(solution)/shard_map/while/body/eval_jaxpr/ppermute | solution.py:21
  224.6 7.0 %collective-permute-start = (f32[1,16,128]{2,1,0:T(8,128)S(1)}, f32[1,16,128]{2,1,0:T(8,128)S(1)}, u32[]{:S(2)}, u32[]{:S(2)}) collective-permute-start(f32[1,16,128]{2,1,0:T(8,128)S(1)} %get-tuple-element.271), channel_id=1, source_target_pairs={{0,64},{64,128},{128,192},{192,256},{256,320},{320,384},{384,448},... | collective-permute-start | bytes 24584 | tf_op jit(solution)/shard_map/while/body/eval_jaxpr/ppermute | solution.py:21
  224.6 7.2 %collective-permute-start.1 = (f32[1,16,128]{2,1,0:T(8,128)S(1)}, f32[1,16,128]{2,1,0:T(8,128)S(1)}, u32[]{:S(2)}, u32[]{:S(2)}) collective-permute-start(f32[1,16,128]{2,1,0:T(8,128)S(1)} %get-tuple-element.272), channel_id=1, source_target_pairs={{64,0},{128,64},{192,128},{256,192},{320,256},{384,320},{448,384},... | collective-permute-start | bytes 24584 | tf_op jit(solution)/shard_map/while/body/eval_jaxpr/ppermute | solution.py:22
  233.7 5.6 collective-permute-start.3
  241.3 6.3 %collective-permute-start.5 = (f32[6,18,1]{2,1,0:T(8,128)S(1)}, f32[6,18,1]{2,1,0:T(8,128)S(1)}, u32[]{:S(2)}, u32[]{:S(2)}) collective-permute-start(f32[6,18,1]{2,1,0:T(8,128)S(1)} %get-tuple-element.276), channel_id=1, source_target_pairs={{0,1},{1,2},{2,3},{3,4},{4,5},{5,6},{6,7},{7,0},{8,9},{9,10},{10,1... | collective-permute-start | bytes 1304 | tf_op jit(solution)/shard_map/while/body/eval_jaxpr/ppermute | solution.py:21
  247.9 6.7 %collective-permute-start = (f32[1,16,128]{2,1,0:T(8,128)S(1)}, f32[1,16,128]{2,1,0:T(8,128)S(1)}, u32[]{:S(2)}, u32[]{:S(2)}) collective-permute-start(f32[1,16,128]{2,1,0:T(8,128)S(1)} %get-tuple-element.271), channel_id=1, source_target_pairs={{0,64},{64,128},{128,192},{192,256},{256,320},{320,384},{384,448},... | collective-permute-start | bytes 24584 | tf_op jit(solution)/shard_map/while/body/eval_jaxpr/ppermute | solution.py:21
  248.0 6.8 %collective-permute-start.1 = (f32[1,16,128]{2,1,0:T(8,128)S(1)}, f32[1,16,128]{2,1,0:T(8,128)S(1)}, u32[]{:S(2)}, u32[]{:S(2)}) collective-permute-start(f32[1,16,128]{2,1,0:T(8,128)S(1)} %get-tuple-element.272), channel_id=1, source_target_pairs={{64,0},{128,64},{192,128},{256,192},{320,256},{384,320},{448,384},... | collective-permute-start | bytes 24584 | tf_op jit(solution)/shard_map/while/body/eval_jaxpr/ppermute | solution.py:22
  256.7 5.6 collective-permute-start.3
  264.3 6.3 %collective-permute-start.5 = (f32[6,18,1]{2,1,0:T(8,128)S(1)}, f32[6,18,1]{2,1,0:T(8,128)S(1)}, u32[]{:S(2)}, u32[]{:S(2)}) collective-permute-start(f32[6,18,1]{2,1,0:T(8,128)S(1)} %get-tuple-element.276), channel_id=1, source_target_pairs={{0,1},{1,2},{2,3},{3,4},{4,5},{5,6},{6,7},{7,0},{8,9},{9,10},{10,1... | collective-permute-start | bytes 1304 | tf_op jit(solution)/shard_map/while/body/eval_jaxpr/ppermute | solution.py:21
  271.0 6.7 %collective-permute-start = (f32[1,16,128]{2,1,0:T(8,128)S(1)}, f32[1,16,128]{2,1,0:T(8,128)S(1)}, u32[]{:S(2)}, u32[]{:S(2)}) collective-permute-start(f32[1,16,128]{2,1,0:T(8,128)S(1)} %get-tuple-element.271), channel_id=1, source_target_pairs={{0,64},{64,128},{128,192},{192,256},{256,320},{320,384},{384,448},... | collective-permute-start | bytes 24584 | tf_op jit(solution)/shard_map/while/body/eval_jaxpr/ppermute | solution.py:21
  271.0 6.8 %collective-permute-start.1 = (f32[1,16,128]{2,1,0:T(8,128)S(1)}, f32[1,16,128]{2,1,0:T(8,128)S(1)}, u32[]{:S(2)}, u32[]{:S(2)}) collective-permute-start(f32[1,16,128]{2,1,0:T(8,128)S(1)} %get-tuple-element.272), channel_id=1, source_target_pairs={{64,0},{128,64},{192,128},{256,192},{320,256},{384,320},{448,384},... | collective-permute-start | bytes 24584 | tf_op jit(solution)/shard_map/while/body/eval_jaxpr/ppermute | solution.py:22
  279.8 5.6 collective-permute-start.3
  287.3 6.3 %collective-permute-start.5 = (f32[6,18,1]{2,1,0:T(8,128)S(1)}, f32[6,18,1]{2,1,0:T(8,128)S(1)}, u32[]{:S(2)}, u32[]{:S(2)}) collective-permute-start(f32[6,18,1]{2,1,0:T(8,128)S(1)} %get-tuple-element.276), channel_id=1, source_target_pairs={{0,1},{1,2},{2,3},{3,4},{4,5},{5,6},{6,7},{7,0},{8,9},{9,10},{10,1... | collective-permute-start | bytes 1304 | tf_op jit(solution)/shard_map/while/body/eval_jaxpr/ppermute | solution.py:21
  (29 other events, 690.4 us)
where the time goes:
time: 565 us; the launch traced here: 562 us
  starting transfers between devices  214 us (38%)
  between operations  140 us (25%)
  blocking collectives  115 us (20%)
  waiting for transfers between devices  72.1 us (13%)
  local copies, waits for them, and re-layouts  10.2 us (2%)
    ppermute x36, starting transfers between devices, padded(): after = lax.ppermute(first, axis, down)  127 us
    psum x1, blocking collectives, per_device(): lax.psum((jnp.dot(flat_s, flat_y.T, precision=highest, preferred_element_...  115 us
    ppermute x36, starting transfers between devices, padded(): before = lax.ppermute(last, axis, up)  86.9 us
    ppermute x36, waiting for transfers between devices, padded(): before = lax.ppermute(last, axis, up)  69.9 us
  transfers between devices with their start and end apart: 72, of which 48 were waited for; matrix products, arithmetic and copies ran while one was open for 0% of the time, Pallas kernels for 0%

commit v1 on v0

v1 whole, which is shorter than its diff:
```python
import functools

import jax
import jax.numpy as jnp
from jax import lax
from jax.experimental import pallas as pl
from jax.experimental.pallas import tpu as pltpu
from jax.sharding import PartitionSpec as P

STEPS = 12
AXES = ("rad", "lat", "lon")
MESH = pl.DeviceIdType.MESH

RAD, LAT, LON = 4, 16, 128
WIDE = 12
GROUP = 16
radial_weight = 0.05
latitude_weight = 0.15
longitude_weight = 0.25
F32 = jnp.float32


def ordered(n):
    return sorted(range(1, n), key=lambda d: -min(d, n - d))


def kernel(sizes, g_hbm, k_hbm, s_hbm, y_hbm, smooth_ref, dir_ref, raw, hist, packs, ua, ka, ub, x2a, x2b, x2c, x3a, x3b, x3c,
           gram_send, gram_recv, b_recv, coef, load_sem, send_sem, recv_sem, gs_sem, gr_sem, bs_sem, br_sem):
    n_rad, n_lat, n_lon = sizes
    pairs = s_hbm.shape[0]
    me = tuple(lax.axis_index(a) for a in AXES)

    def peer(*offset):
        return tuple(lax.rem(m + (o % n), n) if o % n else m for m, o, n in zip(me, offset, sizes))

    started = []

    def send(src, dst, ssem, rsem, target):
        copy = pltpu.make_async_remote_copy(src_ref=src, dst_ref=dst, send_sem=ssem, recv_sem=rsem, device_id=target,
                                            device_id_type=MESH)
        copy.start()
        started.append(copy)
        return copy

    load_g = pltpu.make_async_copy(g_hbm, raw.at[0, pl.ds(RAD, RAD), pl.ds(0, LAT)], load_sem.at[0])
    load_k = pltpu.make_async_copy(k_hbm, raw.at[1, pl.ds(RAD, RAD), pl.ds(0, LAT)], load_sem.at[1])
    load_s = pltpu.make_async_copy(s_hbm, hist.at[0], load_sem.at[2])
    load_y = pltpu.make_async_copy(y_hbm, hist.at[1], load_sem.at[3])
    for copy in (load_g, load_k, load_s, load_y):
        copy.start()

    plane = [(a, o) for a in (-1, 0, 1) for o in (-1, 0, 1) if (a, o) != (0, 0)]
    partners = {(0, a % n_lat, o % n_lon) for a, o in plane}
    partners |= {(d, 0, 0) for d in range(1, n_rad)}
    partners |= {(0, d, 0) for d in range(1, n_lat)}
    partners |= {(0, 0, d) for d in range(1, n_lon)}
    partners = sorted(partners)
    barrier = pltpu.get_barrier_semaphore()
    for offset in partners:
        pl.semaphore_signal(barrier, inc=1, device_id=peer(*offset), device_id_type=MESH)

    lane = lax.broadcasted_iota(jnp.int32, (8, LON), 1)
    sub = lax.broadcasted_iota(jnp.int32, (8, LON), 0)

    load_g.wait()
    load_k.wait()
    to_right = jnp.zeros((2, 8, LON), F32)
    to_left = jnp.zeros((2, 8, LON), F32)
    for spot in range(2 * RAD):
        tile = raw[:, RAD + spot // 2, pl.ds(8 * (spot % 2), 8), :]
        here = (lane // GROUP == spot)[None]
        to_right = jnp.where(here, pltpu.roll(tile, (GROUP * spot + GROUP) % LON, 2), to_right)
        to_left = jnp.where(here, pltpu.roll(tile, GROUP * spot, 2) if spot else tile, to_left)
    packs[1, 1, 0] = to_right
    packs[1, 0, 0] = to_left

    pl.semaphore_wait(barrier, len(partners))

    arrive = []
    order = [(a, o) for a in (-1, 1, 0) for o in (-1, 1)]
    for number, (a, o) in enumerate(order):
        side = 1 if o == 1 else 0
        arrive.append(send(packs.at[1, side, 0], packs.at[1, side, 2 + a], send_sem.at[number], recv_sem.at[number],
                           peer(0, a, o)))
    own = pl.ds(RAD, RAD)
    for number, a, first, to in ((6, -1, 0, LAT), (7, 1, LAT - WIDE, LAT + WIDE)):
        arrive.append(send(raw.at[:, own, pl.ds(first, WIDE)], raw.at[:, own, pl.ds(to, WIDE)], send_sem.at[number],
                           recv_sem.at[number], peer(0, a, 0)))
    ends = ((1, 0), (-1, 2 * RAD))
    faces = []
    for number, (r, to) in enumerate(ends):
        faces.append(send(raw.at[:, own, pl.ds(0, LAT)], raw.at[:, pl.ds(to, RAD), pl.ds(0, LAT)], send_sem.at[8 + number],
                          recv_sem.at[8 + number], peer(r, 0, 0)))

    load_s.wait()
    load_y.wait()
    wide_lane = lane[None]
    total = jnp.zeros((pairs, 8, LON), F32)
    for j in range(pairs):
        acc_s = jnp.zeros((pairs, 8, LON), F32)
        acc_y = jnp.zeros((pairs, 8, LON), F32)
        for spot in range(2 * RAD):
            rows = pl.ds(8 * (spot % 2), 8)
            one = hist[1, j, spot // 2, rows, :][None]
            acc_s += hist[0, :, spot // 2, rows, :] * one
            acc_y += hist[1, :, spot // 2, rows, :] * one
        total = jnp.where(wide_lane == j, jnp.sum(acc_s, axis=2, keepdims=True), total)
        total = jnp.where(wide_lane == GROUP + j, jnp.sum(acc_y, axis=2, keepdims=True), total)
    gram_send[0] = jnp.zeros((16, LON), F32)
    gram_send[0, pl.ds(0, pairs)] = jnp.sum(total, axis=1)

    for copy in arrive[6:]:
        copy.wait_recv()
    ring = pl.ds(LAT, 2 * WIDE)
    for number, (r, to) in enumerate(ends):
        faces.append(send(raw.at[:, own, ring], raw.at[:, pl.ds(to, RAD), ring], send_sem.at[10 + number],
                          recv_sem.at[10 + number], peer(r, 0, 0)))
    for copy in arrive[:6]:
        copy.wait_recv()
    for number, (r, to) in enumerate(ends):
        faces.append(send(packs.at[1, :, pl.ds(1, 3)], packs.at[to // RAD, :, pl.ds(1, 3)], send_sem.at[12 + number],
                          recv_sem.at[12 + number], peer(r, 0, 0)))

    def gram_start(stage):
        n = sizes[stage]
        copies = []
        for d in ordered(n):
            offset = [0, 0, 0]
            offset[stage] = d
            copies.append(send(gram_send.at[stage_slot[stage]], gram_recv.at[stage, d - 1], gs_sem.at[stage, d - 1],
                               gr_sem.at[stage, d - 1], peer(*offset)))
        return copies

    stage_slot = {1: 0, 2: 1, 0: 2}

    def gram_end(stage, copies):
        for copy in copies:
            copy.wait_recv()
        return gram_send[stage_slot[stage]] + jnp.sum(gram_recv[stage, pl.ds(0, sizes[stage] - 1)], axis=0)

    gram_copies = gram_start(1)

    for copy in faces:
        copy.wait_recv()

    low_rad = (me[0] > 0).astype(F32)
    high_rad = (me[0] < n_rad - 1).astype(F32)
    low_lat = (me[1] > 0).astype(F32)
    high_lat = (me[1] < n_lat - 1).astype(F32)
    tile_masks = (1.0, 1.0, high_lat, jnp.where(sub < 4, high_lat, low_lat), low_lat)
    for block, rad_mask in ((0, low_rad), (1, 1.0), (2, high_rad)):
        halo = []
        for slot in (1, 2, 3):
            right, left = packs[block, 0, slot], packs[block, 1, slot]
            tiles = []
            for spot in range(2 * RAD):
                a = pltpu.roll(right, (LON - GROUP * spot) % LON, 2) if spot else right
                b = pltpu.roll(left, LON - GROUP - GROUP * spot, 2) if spot < 7 else left
                tiles.append(jnp.where((lane < LON // 2)[None], a, b))
            halo.append(tiles)
        for layer in range(RAD):
            high, mid, low = (halo[s][2 * layer:2 * layer + 2] for s in (0, 1, 2))
            columns = (mid[0], mid[1], high[0], jnp.where((sub < 4)[None], high[1], low[0]), low[1])
            at = RAD * block + layer
            for t in range(5):
                mask = tile_masks[t] * rad_mask
                rows = pl.ds(8 * t, 8)
                main = raw[:, at, rows, :]
                ua[at, rows, pl.ds(0, LON)] = main[0] * mask
                ua[at, rows, pl.ds(LON, LON)] = columns[t][0] * mask
                ka[at, rows, pl.ds(0, LON)] = main[1] * (mask * radial_weight)
                ka[at, rows, pl.ds(LON, LON)] = columns[t][1] * (mask * radial_weight)

    def advance(src, dst, depth, pick, lo, hi):
        rows = src.shape[1]

        def layer(r):
            value = src[r]
            if lo is not None and r < RAD:
                value = value * lo
            if hi is not None and r >= 2 * RAD:
                value = value * hi
            return value

        before, here = layer(depth - 1), layer(depth)
        for r in range(depth, 3 * RAD - depth):
            after = layer(r + 1)
            lat = pltpu.roll(here, 1, 0) + pltpu.roll(here, rows - 1, 0)
            lon = pltpu.roll(here, 1, 1) + pltpu.roll(here, 2 * LON - 1, 1)
            dst(r, here + pick(r) * ((before + after) + 3.0 * lat + (5.0 * lon - 18.0 * here)))
            before, here = here, after

    def store(ref):
        def put(r, value):
            ref[r] = value
        return put

    def pick1(r):
        return ka[r]

    def pick2(r):
        return jnp.concatenate([ka[r, pl.ds(0, 24)], ka[r, pl.ds(32, 8)]], axis=0)

    wide_sub = lax.broadcasted_iota(jnp.int32, (8, 2 * LON), 0)

    def pick3(r):
        seam = jnp.where(wide_sub < 4, ka[r, pl.ds(16, 8)], ka[r, pl.ds(32, 8)])
        return jnp.concatenate([ka[r, pl.ds(0, 16)], seam], axis=0)

    def keep2(r, value):
        x2a[r, pl.ds(0, 24)] = value[0:24]
        x2a[r, pl.ds(24, 8)] = value[32:40]

    def keep3(r, value):
        x3a[r, pl.ds(0, 16)] = value[0:16]
        x3a[r, pl.ds(16, 8)] = jnp.where(wide_sub < 4, value[16:24], value[24:32])

    def exchange(ref, number):
        return [send(ref.at[own], ref.at[pl.ds(to, RAD)], send_sem.at[number + i], recv_sem.at[number + i], peer(r, 0, 0))
                for i, (r, to) in enumerate(ends)]

    advance(ua, store(ub), 1, pick1, None, None)
    advance(ub, store(ua), 2, pick1, None, None)
    advance(ua, store(ub), 3, pick1, None, None)
    advance(ub, keep2, 4, pick1, None, None)
    copies = exchange(x2a, 14)
    gram_send[1] = gram_end(1, gram_copies)
    gram_copies = gram_start(2)
    for copy in copies:
        copy.wait_recv()
    advance(x2a, store(x2b), 1, pick2, low_rad, high_rad)
    advance(x2b, store(x2c), 2, pick2, None, None)
    advance(x2c, store(x2b), 3, pick2, None, None)
    advance(x2b, keep3, 4, pick2, None, None)
    copies = exchange(x3a, 16)
    gram_send[2] = gram_end(2, gram_copies)
    gram_copies = gram_start(0)
    for copy in copies:
        copy.wait_recv()
    advance(x3a, store(x3b), 1, pick3, low_rad, high_rad)
    advance(x3b, store(x3c), 2, pick3, None, None)
    advance(x3c, store(x3b), 3, pick3, None, None)

    def finish(r, value):
        smooth_ref[r - RAD] = value[0:LAT, 0:LON]

    advance(x3b, finish, 4, pick3, None, None)

    acc = [jnp.zeros((pairs, 8, LON), F32) for _ in range(2)]
    for spot in range(2 * RAD):
        rows = pl.ds(8 * (spot % 2), 8)
        field = smooth_ref[spot // 2, rows, :][None]
        acc = [acc[h] + hist[h, :, spot // 2, rows, :] * field for h in range(2)]
    line = jnp.zeros((8, LON), F32)
    for h in range(2):
        sums = jnp.sum(acc[h], axis=2, keepdims=True)
        for i in range(pairs):
            line = jnp.where(lane == GROUP * h + i, sums[i], line)

    def add_up(stage, row):
        b_recv[stage, pl.ds(0, 1)] = row
        copies = []
        for d in ordered(sizes[stage]):
            offset = [0, 0, 0]
            offset[stage] = d
            copies.append(send(b_recv.at[stage, pl.ds(0, 1)], b_recv.at[stage, pl.ds(d, 1)], bs_sem.at[stage, d - 1],
                               br_sem.at[stage, d - 1], peer(*offset)))
        return copies

    def added(stage, copies):
        for copy in copies:
            copy.wait_recv()
        return jnp.sum(b_recv[stage, pl.ds(0, sizes[stage])], axis=0, keepdims=True)

    copies = add_up(1, jnp.sum(line, axis=0, keepdims=True))

    gram = gram_end(0, gram_copies)
    col = lax.broadcasted_iota(jnp.int32, (16, LON), 1)
    row = lax.broadcasted_iota(jnp.int32, (16, LON), 0)
    inside = row < pairs
    diagonal = (col == row) & inside
    d = jnp.sum(jnp.where(diagonal, gram, 0.0), axis=1, keepdims=True)
    inverse = 1.0 / jnp.where(inside[:, 0:1], d, 1.0)
    scaling = gram[pairs - 1:pairs, pairs - 1:pairs] / gram[pairs - 1:pairs, GROUP + pairs - 1:GROUP + pairs]
    upper = jnp.where((col > row) & (col < pairs), gram * inverse, 0.0)
    solve = jnp.where(diagonal, 1.0, 0.0)
    for k in range(pairs - 1, 0, -1):
        solve = solve - upper[:, k:k + 1] * solve[k:k + 1, :]
    inverse_row = jnp.sum(jnp.where(diagonal, inverse, 0.0), axis=0, keepdims=True)
    alpha = solve * inverse_row
    right = d * alpha
    for k in range(pairs):
        right = right + (scaling * gram[:, GROUP + k:GROUP + k + 1]) * alpha[k:k + 1, :]
    right = jnp.where((col == row + GROUP) & inside, -scaling, right)
    for k in range(pairs - 1):
        column = jnp.sum(jnp.where(col == row, upper[k:k + 1, :], 0.0), axis=1, keepdims=True)
        right = right - column * right[k:k + 1, :]
    of_s = -(right * inverse)
    of_y = scaling * alpha

    copies = add_up(2, added(1, copies))
    copies = add_up(0, added(2, copies))
    b = added(0, copies)
    coef[0] = jnp.broadcast_to(jnp.sum(of_s * b, axis=1, keepdims=True), (16, LON))
    coef[1] = jnp.broadcast_to(jnp.sum(of_y * b, axis=1, keepdims=True), (16, LON))
    for spot in range(2 * RAD):
        rows = pl.ds(8 * (spot % 2), 8)
        value = -scaling * smooth_ref[spot // 2, rows, :]
        for i in range(pairs):
            value = value + coef[0, pl.ds(i, 1)] * hist[0, i, spot // 2, rows, :]
            value = value + coef[1, pl.ds(i, 1)] * hist[1, i, spot // 2, rows, :]
        dir_ref[spot // 2, rows, :] = value

    for copy in started:
        copy.wait_send()


def per_device(sizes, gradient, conductance, s_hist, y_hist):
    pairs = s_hist.shape[0]
    most = max(sizes)
    vmem, dma = pltpu.VMEM, pltpu.SemaphoreType.DMA
    shape = jax.ShapeDtypeStruct(gradient.shape, F32)
    return pl.pallas_call(
        functools.partial(kernel, sizes),
        out_shape=(shape, shape),
        in_specs=[pl.BlockSpec(memory_space=pltpu.HBM)] * 4,
        out_specs=(pl.BlockSpec(memory_space=vmem),) * 2,
        scratch_shapes=[
            vmem((2, 3 * RAD, 40, LON), F32),
            vmem((2, pairs, RAD, LAT, LON), F32),
            vmem((3, 2, 4, 2, 8, LON), F32),
            vmem((3 * RAD, 40, 2 * LON), F32),
            vmem((3 * RAD, 40, 2 * LON), F32),
            vmem((3 * RAD, 40, 2 * LON), F32),
            vmem((3 * RAD, 32, 2 * LON), F32),
            vmem((3 * RAD, 32, 2 * LON), F32),
            vmem((3 * RAD, 32, 2 * LON), F32),
            vmem((3 * RAD, 24, 2 * LON), F32),
            vmem((3 * RAD, 24, 2 * LON), F32),
            vmem((3 * RAD, 24, 2 * LON), F32),
            vmem((3, 16, LON), F32),
            vmem((3, most - 1, 16, LON), F32),
            vmem((3, 16, LON), F32),
            vmem((2, 16, LON), F32),
            dma((4,)),
            dma((18,)),
            dma((18,)),
            dma((3, most - 1)),
            dma((3, most - 1)),
            dma((3, most - 1)),
            dma((3, most - 1)),
        ],
        compiler_params=pltpu.CompilerParams(collective_id=0, has_side_effects=True, vmem_limit_bytes=60 * 2**20),
        cost_estimate=pl.CostEstimate(flops=20_000_000, bytes_accessed=800_000, transcendentals=0),
        name="filter_and_direction",
    )(gradient, conductance, s_hist, y_hist)


def solution(mesh):
    sizes = tuple(mesh.shape[a] for a in AXES)
    field, history = P(*AXES), P(None, *AXES)
    return jax.shard_map(
        functools.partial(per_device, sizes),
        mesh=mesh,
        in_specs=(field, field, history, history),
        out_specs=(field, field),
        check_vma=False,
    )
```

time: 565 us -> 62.6 us (0.11)
  starting transfers between devices: 214 us -> 0 us
  between operations: 140 us -> 0.65 us
  blocking collectives: 115 us -> 0 us
  waiting for transfers between devices: 72.1 us -> 0 us
  Pallas kernels: 0 us -> 59.7 us
  local copies, waits for them, and re-layouts: 10.2 us -> 2 us
    ppermute x72 -> x0, starting transfers between devices: 214 us -> none  [the longest x36 127 us: padded(): after = lax.ppermute(first, axis, down)]
    psum x1 -> x0, blocking collectives: 115 us -> none  [per_device(): lax.psum((jnp.dot(flat_s, flat_y.T, precision=highest, preferred_element_...]
    ppermute x72 -> x0, waiting for transfers between devices: 72.1 us -> none  [the longest x36 69.9 us: padded(): before = lax.ppermute(last, axis, up)]
    pallas_call x0 -> x1, Pallas kernels: none -> 59.7 us  [per_device(): pl.pallas_call(functools.partial(kernel, sizes), out_shape=(shape, shape)...]
    slice x47 -> x0, local copies, waits for them, and re-layouts: 8.98 us -> none  [the longest x6 4.34 us: coefficients(): total = total - scaling * alphas[other] * pair_yy[position, other]]
  transfers between devices with their start and end apart: 72 -> 0, of which waited for: 48 -> 0; matrix products, arithmetic and copies ran while one was open for 0% -> 0% of each run, Pallas kernels for 0% -> 0%
where the time goes in v1:
time: 62.6 us; the launch traced here: 62.4 us
  Pallas kernels  59.7 us (95%)
  local copies, waits for them, and re-layouts  2 us (3%)
  between operations  0.65 us (1%)
    pallas_call x1, Pallas kernels, per_device(): pl.pallas_call(functools.partial(kernel, sizes), out_shape=(shape, shape)...  59.7 us
    unnamed x4, local copies, waits for them, and re-layouts  2 us

profile of v1, /device:TPU:1, one launch (start us, length us, event | category | flops | bytes accessed | tf_op | source)
XLA Modules:
  0.0 62.4 jit_solution(11852061699682934921)
XLA Ops:
  0.6 59.7 %filter_and_direction.1 = (f32[4,16,128]{2,1,0:T(8,128)}, f32[4,16,128]{2,1,0:T(8,128)}) custom-call(f32[4,16,128]{2,1,0:T(8,128)} %g_hbm.1, f32[4,16,128]{2,1,0:T(8,128)} %k_hbm.1, f32[10,4,16,128]{3,2,1,0:T(8,128)} %s_hbm.1, f32[10,4,16,128]{3,2,1,0:T(8,128)} %y_hbm.1), custom_call_target="tpu_custom_call" | custom-call | flops 20000000 | bytes 800000 | tf_op jit(solution)/shard_map/filter_and_direction/pallas_call | solution.py:323
  60.4 0.0 copy-start
  60.4 1.4 %copy.8 = f32[4,16,128]{2,1,0:T(8,128)} copy(f32[4,16,128]{2,1,0:T(8,128)} %get-tuple-element.4) | data formatting | bytes 65536
  61.8 0.0 copy-done
  61.8 0.6 copy.9
Async XLA Ops:
  60.4 1.4 %copy-start = (f32[4,16,128]{2,1,0:T(8,128)S(1)}, f32[4,16,128]{2,1,0:T(8,128)}, u32[]{:S(2)}) copy-start(f32[4,16,128]{2,1,0:T(8,128)} %get-tuple-element.5) | copy-start | bytes 98308

commit v2 on v1

v2 whole, which is shorter than its diff:
```python
import functools

import jax
import jax.numpy as jnp
from jax import lax
from jax.experimental import pallas as pl
from jax.experimental.pallas import tpu as pltpu
from jax.sharding import PartitionSpec as P

STEPS = 12
AXES = ("rad", "lat", "lon")
MESH = pl.DeviceIdType.MESH

RAD, LAT, LON = 4, 16, 128
WIDE = 12
GROUP = 16
radial_weight = 0.05
latitude_weight = 0.15
longitude_weight = 0.25
F32 = jnp.float32


def ordered(n):
    return sorted(range(1, n), key=lambda d: -min(d, n - d))


def kernel(sizes, g_hbm, k_hbm, s_hbm, y_hbm, smooth_ref, dir_ref, raw, hist, edges, packs, ua, ka, ub, x2a, x2b, x2c, x3a,
           x3b, x3c, gram_send, gram_recv, plane_row, rad_row, coef, load_sem, halo_sent, halo_here, face_sent, face_here,
           gram_sent, gram_here, row_sent, row_here, near_in, far_in):
    n_rad, n_lat, n_lon = sizes
    pairs = s_hbm.shape[0]
    me = tuple(lax.axis_index(a) for a in AXES)

    def peer(*offset):
        return tuple(lax.rem(m + (o % n), n) if o % n else m for m, o, n in zip(me, offset, sizes))

    owed = []

    def send(src, dst, ssem, rsem, target):
        pltpu.make_async_remote_copy(src_ref=src, dst_ref=dst, send_sem=ssem, recv_sem=rsem, device_id=target,
                                     device_id_type=MESH).start()

    def wait_bytes(ref, sem):
        pltpu.make_async_copy(ref, ref, sem).wait()

    load_g = pltpu.make_async_copy(g_hbm, raw.at[0, pl.ds(RAD, RAD), pl.ds(0, LAT)], load_sem.at[0])
    load_k = pltpu.make_async_copy(k_hbm, raw.at[1, pl.ds(RAD, RAD), pl.ds(0, LAT)], load_sem.at[1])
    load_s = pltpu.make_async_copy(s_hbm, hist.at[0], load_sem.at[2])
    load_y = pltpu.make_async_copy(y_hbm, hist.at[1], load_sem.at[3])
    for copy in (load_g, load_k, load_s, load_y):
        copy.start()

    near = (0, -1, 1)
    cube = [(r, a, o) for r in near for a in near for o in near][1:]
    cube.sort(key=lambda c: -sum(map(abs, c)))
    barrier = pltpu.get_barrier_semaphore()
    for offset in cube:
        pl.semaphore_signal(barrier, inc=1, device_id=peer(*offset), device_id_type=MESH)

    lane = lax.broadcasted_iota(jnp.int32, (8, LON), 1)
    sub = lax.broadcasted_iota(jnp.int32, (8, LON), 0)

    load_g.wait()
    load_k.wait()
    to_right = jnp.zeros((2, 8, LON), F32)
    to_left = jnp.zeros((2, 8, LON), F32)
    for spot in range(2 * RAD):
        tile = raw[:, RAD + spot // 2, pl.ds(8 * (spot % 2), 8), :]
        here = (lane // GROUP == spot)[None]
        to_right = jnp.where(here, pltpu.roll(tile, (GROUP * spot + GROUP) % LON, 2), to_right)
        to_left = jnp.where(here, pltpu.roll(tile, GROUP * spot, 2) if spot else tile, to_left)
    edges[0] = to_left
    edges[1] = to_right

    pl.semaphore_wait(barrier, len(cube))

    own = pl.ds(RAD, RAD)

    def block_of(r):
        return 1 - r

    rows_of = {-1: (0, WIDE, LAT), 0: (0, LAT, 0), 1: (LAT - WIDE, WIDE, LAT + WIDE)}

    def halo(r, a, o):
        at = block_of(r)
        if o:
            side = (o + 1) // 2
            send(edges.at[side], packs.at[at, side, 1 + a], halo_sent.at[3], halo_here.at[3], peer(r, a, o))
        else:
            first, count, to = rows_of[a]
            send(raw.at[:, own, pl.ds(first, count)], raw.at[:, pl.ds(RAD * at, RAD), pl.ds(to, count)], halo_sent.at[at],
                 halo_here.at[at], peer(r, a, o))

    for offset in cube:
        halo(*offset)
    halos = ((raw.at[:, pl.ds(0, RAD)], 0), (raw.at[:, own, pl.ds(LAT, 2 * WIDE)], 1), (raw.at[:, pl.ds(2 * RAD, RAD)], 2),
             (packs, 3))
    owed += [(ref, halo_sent.at[number]) for ref, number in halos]

    load_s.wait()
    load_y.wait()
    total = [jnp.zeros((8, LON), F32) for _ in range(-(-pairs // 4))]
    for j in range(pairs):
        acc_s = jnp.zeros((pairs, 8, LON), F32)
        acc_y = jnp.zeros((pairs, 8, LON), F32)
        for spot in range(2 * RAD):
            rows = pl.ds(8 * (spot % 2), 8)
            one = hist[1, j, spot // 2, rows, :][None]
            acc_s += hist[0, :, spot // 2, rows, :] * one
            acc_y += hist[1, :, spot // 2, rows, :] * one
        sum_s = jnp.sum(acc_s, axis=2, keepdims=True)
        sum_y = jnp.sum(acc_y, axis=2, keepdims=True)
        for i in range(pairs):
            at = 32 * (i % 4) + j
            total[i // 4] = jnp.where(lane == at, sum_s[i], jnp.where(lane == at + GROUP, sum_y[i], total[i // 4]))
    for line, value in enumerate(total):
        gram_send[0, pl.ds(line, 1)] = jnp.sum(value, axis=0, keepdims=True)
    lines = pl.ds(0, len(total))

    for ref, number in halos:
        wait_bytes(ref, halo_here.at[number])

    signs = (0, -2, 2)
    outer = [(0, a, o) for a in signs for o in signs][1:] + [(-2, 0, 0), (2, 0, 0)]
    for offset in outer:
        pl.semaphore_signal(near_in, inc=1, device_id=peer(*offset), device_id_type=MESH)

    turn = {1: 0, 2: 1, 0: 2}

    def gram_start(stage):
        at = turn[stage]
        for d in ordered(sizes[stage]):
            offset = [0, 0, 0]
            offset[stage] = d
            send(gram_send.at[at, lines], gram_recv.at[at, d - 1, lines], gram_sent.at[at], gram_here.at[at], peer(*offset))
        owed.append((gram_recv.at[at, pl.ds(0, sizes[stage] - 1), lines], gram_sent.at[at]))

    def gram_end(stage):
        at = turn[stage]
        ref = gram_recv.at[at, pl.ds(0, sizes[stage] - 1), lines]
        wait_bytes(ref, gram_here.at[at])
        return gram_send[at, lines] + jnp.sum(gram_recv[at, pl.ds(0, sizes[stage] - 1), lines], axis=0)

    low_rad = (me[0] > 0).astype(F32)
    high_rad = (me[0] < n_rad - 1).astype(F32)
    low_lat = (me[1] > 0).astype(F32)
    high_lat = (me[1] < n_lat - 1).astype(F32)
    tile_masks = (1.0, 1.0, high_lat, jnp.where(sub < 4, high_lat, low_lat), low_lat)
    for block, rad_mask in ((0, low_rad), (1, 1.0), (2, high_rad)):
        sides = []
        for slot in range(3):
            right, left = packs[block, 0, slot], packs[block, 1, slot]
            tiles = []
            for spot in range(2 * RAD):
                a = pltpu.roll(right, (LON - GROUP * spot) % LON, 2) if spot else right
                b = pltpu.roll(left, LON - GROUP - GROUP * spot, 2) if spot < 7 else left
                tiles.append(jnp.where((lane < LON // 2)[None], a, b))
            sides.append(tiles)
        for layer in range(RAD):
            high, mid, low = (sides[s][2 * layer:2 * layer + 2] for s in (0, 1, 2))
            columns = (mid[0], mid[1], high[0], jnp.where((sub < 4)[None], high[1], low[0]), low[1])
            at = RAD * block + layer
            for t in range(5):
                mask = tile_masks[t] * rad_mask
                rows = pl.ds(8 * t, 8)
                main = raw[:, at, rows, :]
                ua[at, rows, pl.ds(0, LON)] = main[0] * mask
                ua[at, rows, pl.ds(LON, LON)] = columns[t][0] * mask
                ka[at, rows, pl.ds(0, LON)] = main[1] * (mask * radial_weight)
                ka[at, rows, pl.ds(LON, LON)] = columns[t][1] * (mask * radial_weight)

    def advance(src, dst, depth, pick, lo, hi):
        rows = src.shape[1]

        def layer(r):
            value = src[r]
            if lo is not None and r < RAD:
                value = value * lo
            if hi is not None and r >= 2 * RAD:
                value = value * hi
            return value

        before, here = layer(depth - 1), layer(depth)
        for r in range(depth, 3 * RAD - depth):
            after = layer(r + 1)
            lat = pltpu.roll(here, 1, 0) + pltpu.roll(here, rows - 1, 0)
            lon = pltpu.roll(here, 1, 1) + pltpu.roll(here, 2 * LON - 1, 1)
            dst(r, here + pick(r) * ((before + after) + 3.0 * lat + (5.0 * lon - 18.0 * here)))
            before, here = here, after

    def store(ref):
        def put(r, value):
            ref[r] = value
        return put

    def pick1(r):
        return ka[r]

    def pick2(r):
        return jnp.concatenate([ka[r, pl.ds(0, 24)], ka[r, pl.ds(32, 8)]], axis=0)

    wide_sub = lax.broadcasted_iota(jnp.int32, (8, 2 * LON), 0)

    def pick3(r):
        seam = jnp.where(wide_sub < 4, ka[r, pl.ds(16, 8)], ka[r, pl.ds(32, 8)])
        return jnp.concatenate([ka[r, pl.ds(0, 16)], seam], axis=0)

    def keep2(r, value):
        x2a[r, pl.ds(0, 24)] = value[0:24]
        x2a[r, pl.ds(24, 8)] = value[32:40]

    def keep3(r, value):
        x3a[r, pl.ds(0, 16)] = value[0:16]
        x3a[r, pl.ds(16, 8)] = jnp.where(wide_sub < 4, value[16:24], value[24:32])

    def exchange(ref, number):
        for r in (1, -1):
            send(ref.at[own], ref.at[pl.ds(RAD * block_of(r), RAD)], face_sent.at[number], face_here.at[number], peer(r, 0, 0))
        owed.append((ref.at[pl.ds(0, 2 * RAD)], face_sent.at[number]))

    def exchanged(ref, number):
        wait_bytes(ref.at[pl.ds(0, 2 * RAD)], face_here.at[number])

    advance(ua, store(ub), 1, pick1, None, None)
    advance(ub, store(ua), 2, pick1, None, None)
    advance(ua, store(ub), 3, pick1, None, None)
    advance(ub, keep2, 4, pick1, None, None)
    exchange(x2a, 0)
    pl.semaphore_wait(near_in, len(outer))
    for r in (-4, 4):
        pl.semaphore_signal(far_in, inc=1, device_id=peer(r, 0, 0), device_id_type=MESH)
    gram_start(1)
    exchanged(x2a, 0)
    advance(x2a, store(x2b), 1, pick2, low_rad, high_rad)
    advance(x2b, store(x2c), 2, pick2, None, None)
    advance(x2c, store(x2b), 3, pick2, None, None)
    advance(x2b, keep3, 4, pick2, None, None)
    exchange(x3a, 1)
    pl.semaphore_wait(far_in, 2)
    exchanged(x3a, 1)
    gram_send[1, lines] = gram_end(1)
    gram_start(2)
    advance(x3a, store(x3b), 1, pick3, low_rad, high_rad)
    advance(x3b, store(x3c), 2, pick3, None, None)
    advance(x3c, store(x3b), 3, pick3, None, None)

    def finish(r, value):
        smooth_ref[r - RAD] = value[0:LAT, 0:LON]

    advance(x3b, finish, 4, pick3, None, None)

    acc = [jnp.zeros((pairs, 8, LON), F32) for _ in range(2)]
    for spot in range(2 * RAD):
        rows = pl.ds(8 * (spot % 2), 8)
        field = smooth_ref[spot // 2, rows, :][None]
        acc = [acc[h] + hist[h, :, spot // 2, rows, :] * field for h in range(2)]
    line = jnp.zeros((8, LON), F32)
    for h in range(2):
        sums = jnp.sum(acc[h], axis=2, keepdims=True)
        for i in range(pairs):
            line = jnp.where(lane == GROUP * h + i, sums[i], line)

    def hops(offset):
        return sum(min(d, n - d) for d, n in zip(offset, sizes))

    def add_up(buf, row, offsets, number):
        count = len(offsets)
        buf[pl.ds(count, 1)] = row
        for at, offset in enumerate(sorted(offsets, key=lambda c: -hops(c))):
            send(buf.at[pl.ds(count, 1)], buf.at[pl.ds(at, 1)], row_sent.at[number], row_here.at[number], peer(*offset))
        owed.append((buf.at[pl.ds(0, count)], row_sent.at[number]))

    def added(buf, offsets, number):
        count = len(offsets)
        wait_bytes(buf.at[pl.ds(0, count)], row_here.at[number])
        return jnp.sum(buf[pl.ds(0, count + 1)], axis=0, keepdims=True)

    in_plane = [(0, a, o) for a in range(n_lat) for o in range(n_lon)][1:]
    in_rad = [(r, 0, 0) for r in range(1, n_rad)]
    add_up(plane_row, jnp.sum(line, axis=0, keepdims=True), in_plane, 0)
    gram_send[2, lines] = gram_end(2)
    gram_start(0)
    add_up(rad_row, added(plane_row, in_plane, 0), in_rad, 1)

    packed = gram_end(0)
    parts = [pltpu.roll(packed[i // 4:i // 4 + 1], LON - 32 * (i % 4), 1) if i % 4 else packed[i // 4:i // 4 + 1]
             for i in range(pairs)]
    gram = jnp.concatenate(parts + [jnp.zeros((16 - pairs, LON), F32)], axis=0)
    col = lax.broadcasted_iota(jnp.int32, (16, LON), 1)
    row = lax.broadcasted_iota(jnp.int32, (16, LON), 0)
    inside = row < pairs
    diagonal = (col == row) & inside
    d = jnp.sum(jnp.where(diagonal, gram, 0.0), axis=1, keepdims=True)
    inverse = 1.0 / jnp.where(inside[:, 0:1], d, 1.0)
    scaling = gram[pairs - 1:pairs, pairs - 1:pairs] / gram[pairs - 1:pairs, GROUP + pairs - 1:GROUP + pairs]
    upper = jnp.where((col > row) & (col < pairs), gram * inverse, 0.0)
    solve = jnp.where(diagonal, 1.0, 0.0)
    for k in range(pairs - 1, 0, -1):
        solve = solve - upper[:, k:k + 1] * solve[k:k + 1, :]
    inverse_row = jnp.sum(jnp.where(diagonal, inverse, 0.0), axis=0, keepdims=True)
    alpha = solve * inverse_row
    right = d * alpha
    for k in range(pairs):
        right = right + (scaling * gram[:, GROUP + k:GROUP + k + 1]) * alpha[k:k + 1, :]
    right = jnp.where((col == row + GROUP) & inside, -scaling, right)
    for k in range(pairs - 1):
        column = jnp.sum(jnp.where(col == row, upper[k:k + 1, :], 0.0), axis=1, keepdims=True)
        right = right - column * right[k:k + 1, :]
    of_s = -(right * inverse)
    of_y = scaling * alpha

    b = added(rad_row, in_rad, 1)
    coef[0] = jnp.broadcast_to(jnp.sum(of_s * b, axis=1, keepdims=True), (16, LON))
    coef[1] = jnp.broadcast_to(jnp.sum(of_y * b, axis=1, keepdims=True), (16, LON))
    for spot in range(2 * RAD):
        rows = pl.ds(8 * (spot % 2), 8)
        value = -scaling * smooth_ref[spot // 2, rows, :]
        for i in range(pairs):
            value = value + coef[0, pl.ds(i, 1)] * hist[0, i, spot // 2, rows, :]
            value = value + coef[1, pl.ds(i, 1)] * hist[1, i, spot // 2, rows, :]
        dir_ref[spot // 2, rows, :] = value

    for ref, sem in owed:
        wait_bytes(ref, sem)


def per_device(sizes, gradient, conductance, s_hist, y_hist):
    pairs = s_hist.shape[0]
    most = max(sizes)
    vmem, dma = pltpu.VMEM, pltpu.SemaphoreType.DMA
    shape = jax.ShapeDtypeStruct(gradient.shape, F32)
    return pl.pallas_call(
        functools.partial(kernel, sizes),
        out_shape=(shape, shape),
        in_specs=[pl.BlockSpec(memory_space=pltpu.HBM)] * 4,
        out_specs=(pl.BlockSpec(memory_space=vmem),) * 2,
        scratch_shapes=[
            vmem((2, 3 * RAD, 40, LON), F32),
            vmem((2, pairs, RAD, LAT, LON), F32),
            vmem((2, 2, 8, LON), F32),
            vmem((3, 2, 3, 2, 8, LON), F32),
            vmem((3 * RAD, 40, 2 * LON), F32),
            vmem((3 * RAD, 40, 2 * LON), F32),
            vmem((3 * RAD, 40, 2 * LON), F32),
            vmem((3 * RAD, 32, 2 * LON), F32),
            vmem((3 * RAD, 32, 2 * LON), F32),
            vmem((3 * RAD, 32, 2 * LON), F32),
            vmem((3 * RAD, 24, 2 * LON), F32),
            vmem((3 * RAD, 24, 2 * LON), F32),
            vmem((3 * RAD, 24, 2 * LON), F32),
            vmem((3, 8, LON), F32),
            vmem((3, most - 1, 8, LON), F32),
            vmem((sizes[1] * sizes[2], LON), F32),
            vmem((sizes[0], LON), F32),
            vmem((2, 16, LON), F32),
            dma((4,)),
            dma((4,)),
            dma((4,)),
            dma((2,)),
            dma((2,)),
            dma((3,)),
            dma((3,)),
            dma((2,)),
            dma((2,)),
            pltpu.SemaphoreType.REGULAR,
            pltpu.SemaphoreType.REGULAR,
        ],
        compiler_params=pltpu.CompilerParams(collective_id=0, has_side_effects=True, vmem_limit_bytes=60 * 2**20),
        cost_estimate=pl.CostEstimate(flops=20_000_000, bytes_accessed=800_000, transcendentals=0),
        name="filter_and_direction",
    )(gradient, conductance, s_hist, y_hist)


def solution(mesh):
    sizes = tuple(mesh.shape[a] for a in AXES)
    field, history = P(*AXES), P(None, *AXES)
    return jax.shard_map(
        functools.partial(per_device, sizes),
        mesh=mesh,
        in_specs=(field, field, history, history),
        out_specs=(field, field),
        check_vma=False,
    )
```

time: 62.6 us -> 52.9 us (0.85)
  Pallas kernels: 59.7 us -> 50 us
    pallas_call x1, Pallas kernels: 59.7 us -> 50 us  [per_device(): pl.pallas_call(functools.partial(kernel, sizes), out_shape=(shape, shape)...]
where the time goes in v2:
time: 52.9 us; the launch traced here: 52.7 us
  Pallas kernels  50 us (95%)
  local copies, waits for them, and re-layouts  2 us (4%)
  between operations  0.65 us (1%)
    pallas_call x1, Pallas kernels, per_device(): pl.pallas_call(functools.partial(kernel, sizes), out_shape=(shape, shape)...  50 us
    unnamed x4, local copies, waits for them, and re-layouts  2 us

profile of v2, /device:TPU:1, one launch (start us, length us, event | category | flops | bytes accessed | tf_op | source)
XLA Modules:
  0.0 52.7 jit_solution(2125647504806819441)
XLA Ops:
  0.6 50.0 %filter_and_direction.1 = (f32[4,16,128]{2,1,0:T(8,128)}, f32[4,16,128]{2,1,0:T(8,128)}) custom-call(f32[4,16,128]{2,1,0:T(8,128)} %g_hbm.1, f32[4,16,128]{2,1,0:T(8,128)} %k_hbm.1, f32[10,4,16,128]{3,2,1,0:T(8,128)} %s_hbm.1, f32[10,4,16,128]{3,2,1,0:T(8,128)} %y_hbm.1), custom_call_target="tpu_custom_call" | custom-call | flops 20000000 | bytes 800000 | tf_op jit(solution)/shard_map/filter_and_direction/pallas_call | solution.py:332
  50.7 0.0 copy-start
  50.7 1.4 %copy.8 = f32[4,16,128]{2,1,0:T(8,128)} copy(f32[4,16,128]{2,1,0:T(8,128)} %get-tuple-element.4) | data formatting | bytes 65536
  52.0 0.0 copy-done
  52.0 0.6 %copy.9 = f32[4,16,128]{2,1,0:T(8,128)} copy(f32[4,16,128]{2,1,0:T(8,128)S(1)} %copy-done) | data formatting | bytes 65536
Async XLA Ops:
  50.7 1.4 %copy-start = (f32[4,16,128]{2,1,0:T(8,128)S(1)}, f32[4,16,128]{2,1,0:T(8,128)}, u32[]{:S(2)}) copy-start(f32[4,16,128]{2,1,0:T(8,128)} %get-tuple-element.5) | copy-start | bytes 98308

commit v3 on v2

--- a/solution.py
+++ b/solution.py
@@ -24,11 +24,12 @@
     return sorted(range(1, n), key=lambda d: -min(d, n - d))
 
 
-def kernel(sizes, g_hbm, k_hbm, s_hbm, y_hbm, smooth_ref, dir_ref, raw, hist, edges, packs, ua, ka, ub, x2a, x2b, x2c, x3a,
+def kernel(sizes, g_hbm, k_hbm, s_hbm, y_hbm, out_ref, raw, hist, edges, packs, ua, ka, ub, x2a, x2b, x2c, x3a,
            x3b, x3c, gram_send, gram_recv, plane_row, rad_row, coef, load_sem, halo_sent, halo_here, face_sent, face_here,
            gram_sent, gram_here, row_sent, row_here, near_in, far_in):
     n_rad, n_lat, n_lon = sizes
     pairs = s_hbm.shape[0]
+    minus_smooth, minus_dir = out_ref.at[0], out_ref.at[1]
     me = tuple(lax.axis_index(a) for a in AXES)
 
     def peer(*offset):
@@ -245,14 +246,14 @@
     advance(x3c, store(x3b), 3, pick3, None, None)
 
     def finish(r, value):
-        smooth_ref[r - RAD] = value[0:LAT, 0:LON]
+        minus_smooth[r - RAD] = -value[0:LAT, 0:LON]
 
     advance(x3b, finish, 4, pick3, None, None)
 
     acc = [jnp.zeros((pairs, 8, LON), F32) for _ in range(2)]
     for spot in range(2 * RAD):
         rows = pl.ds(8 * (spot % 2), 8)
-        field = smooth_ref[spot // 2, rows, :][None]
+        field = -minus_smooth[spot // 2, rows, :][None]
         acc = [acc[h] + hist[h, :, spot // 2, rows, :] * field for h in range(2)]
     line = jnp.zeros((8, LON), F32)
     for h in range(2):
@@ -306,19 +307,19 @@
     for k in range(pairs - 1):
         column = jnp.sum(jnp.where(col == row, upper[k:k + 1, :], 0.0), axis=1, keepdims=True)
         right = right - column * right[k:k + 1, :]
-    of_s = -(right * inverse)
-    of_y = scaling * alpha
+    of_s = right * inverse
+    of_y = -scaling * alpha
 
     b = added(rad_row, in_rad, 1)
     coef[0] = jnp.broadcast_to(jnp.sum(of_s * b, axis=1, keepdims=True), (16, LON))
     coef[1] = jnp.broadcast_to(jnp.sum(of_y * b, axis=1, keepdims=True), (16, LON))
     for spot in range(2 * RAD):
         rows = pl.ds(8 * (spot % 2), 8)
-        value = -scaling * smooth_ref[spot // 2, rows, :]
+        value = -scaling * minus_smooth[spot // 2, rows, :]
         for i in range(pairs):
             value = value + coef[0, pl.ds(i, 1)] * hist[0, i, spot // 2, rows, :]
             value = value + coef[1, pl.ds(i, 1)] * hist[1, i, spot // 2, rows, :]
-        dir_ref[spot // 2, rows, :] = value
+        minus_dir[spot // 2, rows, :] = value
 
     for ref, sem in owed:
         wait_bytes(ref, sem)
@@ -328,12 +329,12 @@
     pairs = s_hist.shape[0]
     most = max(sizes)
     vmem, dma = pltpu.VMEM, pltpu.SemaphoreType.DMA
-    shape = jax.ShapeDtypeStruct(gradient.shape, F32)
-    return pl.pallas_call(
+    inputs = [pltpu.with_memory_space_constraint(a, pltpu.HBM) for a in (gradient, conductance, s_hist, y_hist)]
+    out = pl.pallas_call(
         functools.partial(kernel, sizes),
-        out_shape=(shape, shape),
+        out_shape=pltpu.VMEM((2,) + gradient.shape, F32),
         in_specs=[pl.BlockSpec(memory_space=pltpu.HBM)] * 4,
-        out_specs=(pl.BlockSpec(memory_space=vmem),) * 2,
+        out_specs=pl.BlockSpec(memory_space=vmem),
         scratch_shapes=[
             vmem((2, 3 * RAD, 40, LON), F32),
             vmem((2, pairs, RAD, LAT, LON), F32),
@@ -365,10 +366,11 @@
             pltpu.SemaphoreType.REGULAR,
             pltpu.SemaphoreType.REGULAR,
         ],
-        compiler_params=pltpu.CompilerParams(collective_id=0, has_side_effects=True, vmem_limit_bytes=60 * 2**20),
+        compiler_params=pltpu.CompilerParams(collective_id=0, has_side_effects=True, vmem_limit_bytes=24 * 2**20),
         cost_estimate=pl.CostEstimate(flops=20_000_000, bytes_accessed=800_000, transcendentals=0),
         name="filter_and_direction",
-    )(gradient, conductance, s_hist, y_hist)
+    )(*inputs)
+    return -out[0], -out[1]
 
 
 def solution(mesh):

time: 52.9 us -> 50.8 us (0.960)
  local copies, waits for them, and re-layouts: 2 us -> 0 us
  other arithmetic: 0 us -> 0.63 us
  Pallas kernels: 50 us -> 49.4 us
    unnamed x4 -> x0, local copies, waits for them, and re-layouts: 2 us -> none
    neg x0 -> x1, other arithmetic: none -> 0.63 us  [per_device(): return (-out[0], -out[1])]
    pallas_call x1, Pallas kernels: 50 us -> 49.4 us  [per_device(): pl.pallas_call(functools.partial(kernel, sizes), out_shape=pltpu.VMEM((2,...]
where the time goes in v3:
time: 50.8 us; the launch traced here: 50.7 us
  Pallas kernels  49.4 us (97%)
  between operations  0.64 us (1%)
  other arithmetic  0.63 us (1%)
    pallas_call x1, Pallas kernels, per_device(): pl.pallas_call(functools.partial(kernel, sizes), out_shape=pltpu.VMEM((2,...  49.4 us

profile of v3, /device:TPU:1, one launch (start us, length us, event | category | flops | bytes accessed | tf_op | source)
XLA Modules:
  0.0 50.7 jit_solution(6594293660339984971)
XLA Ops:
  0.6 49.4 %filter_and_direction.1 = f32[2,4,16,128]{3,2,1,0:T(8,128)S(1)} custom-call(f32[4,16,128]{2,1,0:T(8,128)} %g_hbm.1, f32[4,16,128]{2,1,0:T(8,128)} %k_hbm.1, f32[10,4,16,128]{3,2,1,0:T(8,128)} %s_hbm.1, f32[10,4,16,128]{3,2,1,0:T(8,128)} %y_hbm.1), custom_call_target="tpu_custom_call" | custom-call | flops 20000000 | bytes 800000 | tf_op jit(solution)/shard_map/filter_and_direction/pallas_call | solution.py:333
  50.0 0.6 %negate_bitcast_fusion = (f32[4,16,128]{2,1,0:T(8,128)}, f32[4,16,128]{2,1,0:T(8,128)}) fusion(f32[2,4,16,128]{3,2,1,0:T(8,128)S(1)} %filter_and_direction.1), kind=kLoop, calls=%fused_computation | loop fusion | flops 16384 | bytes 131072 | tf_op jit(solution)/shard_map/neg | solution.py:373

commit v4 on v3

--- a/solution.py
+++ b/solution.py
@@ -25,7 +25,7 @@
 
 
 def kernel(sizes, g_hbm, k_hbm, s_hbm, y_hbm, out_ref, raw, hist, edges, packs, ua, ka, ub, x2a, x2b, x2c, x3a,
-           x3b, x3c, gram_send, gram_recv, plane_row, rad_row, coef, load_sem, halo_sent, halo_here, face_sent, face_here,
+           x3b, x3c, side2, side3, gram_send, gram_recv, plane_row, rad_row, coef, load_sem, halo_sent, halo_here, face_sent, face_here,
            gram_sent, gram_here, row_sent, row_here, near_in, far_in):
     n_rad, n_lat, n_lon = sizes
     pairs = s_hbm.shape[0]
@@ -170,11 +170,16 @@
                 ka[at, rows, pl.ds(0, LON)] = main[1] * (mask * radial_weight)
                 ka[at, rows, pl.ds(LON, LON)] = columns[t][1] * (mask * radial_weight)
 
-    def advance(src, dst, depth, pick, lo, hi):
+    def advance(src, dst, depth, pick, lo, hi, sides=None):
         rows = src.shape[1]
 
         def layer(r):
-            value = src[r]
+            if sides is not None and not RAD <= r < 2 * RAD:
+                packed = sides[1 if r < RAD else 2]
+                turn_by = (LON - 32 * (r % RAD)) % LON
+                value = jnp.concatenate([src[r, :, pl.ds(0, LON)], pltpu.roll(packed, turn_by, 1) if turn_by else packed], axis=1)
+            else:
+                value = src[r]
             if lo is not None and r < RAD:
                 value = value * lo
             if hi is not None and r >= 2 * RAD:
@@ -214,34 +219,45 @@
         x3a[r, pl.ds(0, 16)] = value[0:16]
         x3a[r, pl.ds(16, 8)] = jnp.where(wide_sub < 4, value[16:24], value[24:32])
 
-    def exchange(ref, number):
+    def exchange(ref, side, number):
+        main = pl.ds(0, LON)
         for r in (1, -1):
-            send(ref.at[own], ref.at[pl.ds(RAD * block_of(r), RAD)], face_sent.at[number], face_here.at[number], peer(r, 0, 0))
-        owed.append((ref.at[pl.ds(0, 2 * RAD)], face_sent.at[number]))
-
-    def exchanged(ref, number):
-        wait_bytes(ref.at[pl.ds(0, 2 * RAD)], face_here.at[number])
+            send(ref.at[own, :, main], ref.at[pl.ds(RAD * block_of(r), RAD), :, main], face_sent.at[number, 0],
+                 face_here.at[number, 0], peer(r, 0, 0))
+        group = (lax.broadcasted_iota(jnp.int32, side.shape[1:], 1) + GROUP) // 32
+        packed = ref[RAD, :, pl.ds(LON, LON)]
+        for l in range(1, RAD):
+            packed = jnp.where(group == l, pltpu.roll(ref[RAD + l, :, pl.ds(LON, LON)], 32 * l, 1), packed)
+        side[0] = packed
+        for r in (1, -1):
+            send(side.at[0], side.at[1 + block_of(r) // 2], face_sent.at[number, 1], face_here.at[number, 1], peer(r, 0, 0))
+        owed.append((ref.at[pl.ds(0, 2 * RAD), :, main], face_sent.at[number, 0]))
+        owed.append((side.at[pl.ds(1, 2)], face_sent.at[number, 1]))
+
+    def exchanged(ref, side, number):
+        wait_bytes(ref.at[pl.ds(0, 2 * RAD), :, pl.ds(0, LON)], face_here.at[number, 0])
+        wait_bytes(side.at[pl.ds(1, 2)], face_here.at[number, 1])
 
     advance(ua, store(ub), 1, pick1, None, None)
     advance(ub, store(ua), 2, pick1, None, None)
     advance(ua, store(ub), 3, pick1, None, None)
     advance(ub, keep2, 4, pick1, None, None)
-    exchange(x2a, 0)
+    exchange(x2a, side2, 0)
     pl.semaphore_wait(near_in, len(outer))
     for r in (-4, 4):
         pl.semaphore_signal(far_in, inc=1, device_id=peer(r, 0, 0), device_id_type=MESH)
     gram_start(1)
-    exchanged(x2a, 0)
-    advance(x2a, store(x2b), 1, pick2, low_rad, high_rad)
+    exchanged(x2a, side2, 0)
+    advance(x2a, store(x2b), 1, pick2, low_rad, high_rad, side2)
     advance(x2b, store(x2c), 2, pick2, None, None)
     advance(x2c, store(x2b), 3, pick2, None, None)
     advance(x2b, keep3, 4, pick2, None, None)
-    exchange(x3a, 1)
+    exchange(x3a, side3, 1)
     pl.semaphore_wait(far_in, 2)
-    exchanged(x3a, 1)
     gram_send[1, lines] = gram_end(1)
     gram_start(2)
-    advance(x3a, store(x3b), 1, pick3, low_rad, high_rad)
+    exchanged(x3a, side3, 1)
+    advance(x3a, store(x3b), 1, pick3, low_rad, high_rad, side3)
     advance(x3b, store(x3c), 2, pick3, None, None)
     advance(x3c, store(x3b), 3, pick3, None, None)
 
@@ -349,6 +365,8 @@
             vmem((3 * RAD, 24, 2 * LON), F32),
             vmem((3 * RAD, 24, 2 * LON), F32),
             vmem((3 * RAD, 24, 2 * LON), F32),
+            vmem((3, 32, LON), F32),
+            vmem((3, 24, LON), F32),
             vmem((3, 8, LON), F32),
             vmem((3, most - 1, 8, LON), F32),
             vmem((sizes[1] * sizes[2], LON), F32),
@@ -357,8 +375,8 @@
             dma((4,)),
             dma((4,)),
             dma((4,)),
-            dma((2,)),
-            dma((2,)),
+            dma((2, 2)),
+            dma((2, 2)),
             dma((3,)),
             dma((3,)),
             dma((2,)),

time: 50.8 us -> 50.1 us (0.986)
  Pallas kernels: 49.4 us -> 48.7 us
    pallas_call x1, Pallas kernels: 49.4 us -> 48.7 us  [per_device(): pl.pallas_call(functools.partial(kernel, sizes), out_shape=pltpu.VMEM((2,...]
where the time goes in v4:
time: 50.1 us; the launch traced here: 49.9 us
  Pallas kernels  48.7 us (97%)
  between operations  0.64 us (1%)
  other arithmetic  0.63 us (1%)
    pallas_call x1, Pallas kernels, per_device(): pl.pallas_call(functools.partial(kernel, sizes), out_shape=pltpu.VMEM((2,...  48.7 us

profile of v4, /device:TPU:1, one launch (start us, length us, event | category | flops | bytes accessed | tf_op | source)
XLA Modules:
  0.0 49.9 jit_solution(6063932387186866788)
XLA Ops:
  0.6 48.7 %filter_and_direction.1 = f32[2,4,16,128]{3,2,1,0:T(8,128)S(1)} custom-call(f32[4,16,128]{2,1,0:T(8,128)} %g_hbm.1, f32[4,16,128]{2,1,0:T(8,128)} %k_hbm.1, f32[10,4,16,128]{3,2,1,0:T(8,128)} %s_hbm.1, f32[10,4,16,128]{3,2,1,0:T(8,128)} %y_hbm.1), custom_call_target="tpu_custom_call" | custom-call | flops 20000000 | bytes 800000 | tf_op jit(solution)/shard_map/filter_and_direction/pallas_call | solution.py:349
  49.3 0.6 %negate_bitcast_fusion = (f32[4,16,128]{2,1,0:T(8,128)}, f32[4,16,128]{2,1,0:T(8,128)}) fusion(f32[2,4,16,128]{3,2,1,0:T(8,128)S(1)} %filter_and_direction.1), kind=kLoop, calls=%fused_computation | loop fusion | flops 16384 | bytes 131072 | tf_op jit(solution)/shard_map/neg | solution.py:391

commit v5 on v4

--- a/solution.py
+++ b/solution.py
@@ -25,8 +25,8 @@
 
 
 def kernel(sizes, g_hbm, k_hbm, s_hbm, y_hbm, out_ref, raw, hist, edges, packs, ua, ka, ub, x2a, x2b, x2c, x3a,
-           x3b, x3c, side2, side3, gram_send, gram_recv, plane_row, rad_row, coef, load_sem, halo_sent, halo_here, face_sent, face_here,
-           gram_sent, gram_here, row_sent, row_here, near_in, far_in):
+           x3b, x3c, side2, side3, va, vb, near_hist, gram_send, gram_recv, plane_row, rad_row, coef, load_sem, halo_sent, halo_here, face_sent, face_here,
+           gram_sent, gram_here, row_sent, row_here, hist_sent, hist_here, near_in, far_in):
     n_rad, n_lat, n_lon = sizes
     pairs = s_hbm.shape[0]
     minus_smooth, minus_dir = out_ref.at[0], out_ref.at[1]
@@ -100,6 +100,10 @@
 
     load_s.wait()
     load_y.wait()
+    for r in (1, -1):
+        send(hist, near_hist.at[block_of(r) // 2], hist_sent, hist_here, peer(r, 0, 0))
+    owed.append((near_hist, hist_sent))
+
     total = [jnp.zeros((8, LON), F32) for _ in range(-(-pairs // 4))]
     for j in range(pairs):
         acc_s = jnp.zeros((pairs, 8, LON), F32)
@@ -253,24 +257,44 @@
     advance(x2c, store(x2b), 3, pick2, None, None)
     advance(x2b, keep3, 4, pick2, None, None)
     exchange(x3a, side3, 1)
-    pl.semaphore_wait(far_in, 2)
     gram_send[1, lines] = gram_end(1)
     gram_start(2)
-    exchanged(x3a, side3, 1)
-    advance(x3a, store(x3b), 1, pick3, low_rad, high_rad, side3)
-    advance(x3b, store(x3c), 2, pick3, None, None)
-    advance(x3c, store(x3b), 3, pick3, None, None)
-
-    def finish(r, value):
-        minus_smooth[r - RAD] = -value[0:LAT, 0:LON]
-
-    advance(x3b, finish, 4, pick3, None, None)
-
+
+    def spread(src, dst, step):
+        first, last = RAD - step, 2 * RAD - 1 + step
+
+        def layer(r):
+            return src[r] if first < r < last else None
+
+        def plus(a, b):
+            return b if a is None else a if b is None else a + b
+
+        for r in range(first, last + 1):
+            here, around = layer(r), plus(layer(r - 1), layer(r + 1))
+            if here is None:
+                dst[r] = pick3(r) * around
+                continue
+            lat = pltpu.roll(here, 1, 0) + pltpu.roll(here, here.shape[0] - 1, 0)
+            lon = pltpu.roll(here, 1, 1) + pltpu.roll(here, 2 * LON - 1, 1)
+            dst[r] = here + pick3(r) * (around + 3.0 * lat + (5.0 * lon - 18.0 * here))
+
+    spread(x3a, va, 1)
+    spread(va, vb, 2)
+    spread(vb, va, 3)
+    spread(va, vb, 4)
+
+    wait_bytes(near_hist, hist_here)
     acc = [jnp.zeros((pairs, 8, LON), F32) for _ in range(2)]
-    for spot in range(2 * RAD):
-        rows = pl.ds(8 * (spot % 2), 8)
-        field = -minus_smooth[spot // 2, rows, :][None]
-        acc = [acc[h] + hist[h, :, spot // 2, rows, :] * field for h in range(2)]
+    for r in range(3 * RAD):
+        for half in range(LAT // 8):
+            rows = pl.ds(8 * half, 8)
+            field = vb[r, rows, pl.ds(0, LON)][None]
+            for h in range(2):
+                if RAD <= r < 2 * RAD:
+                    values = hist[h, :, r - RAD, rows, :]
+                else:
+                    values = near_hist[r // (2 * RAD), h, :, r % RAD, rows, :]
+                acc[h] = acc[h] + values * field
     line = jnp.zeros((8, LON), F32)
     for h in range(2):
         sums = jnp.sum(acc[h], axis=2, keepdims=True)
@@ -295,8 +319,19 @@
     in_plane = [(0, a, o) for a in range(n_lat) for o in range(n_lon)][1:]
     in_rad = [(r, 0, 0) for r in range(1, n_rad)]
     add_up(plane_row, jnp.sum(line, axis=0, keepdims=True), in_plane, 0)
+    pl.semaphore_wait(far_in, 2)
     gram_send[2, lines] = gram_end(2)
     gram_start(0)
+    exchanged(x3a, side3, 1)
+    advance(x3a, store(x3b), 1, pick3, low_rad, high_rad, side3)
+    advance(x3b, store(x3c), 2, pick3, None, None)
+    advance(x3c, store(x3b), 3, pick3, None, None)
+
+    def finish(r, value):
+        minus_smooth[r - RAD] = -value[0:LAT, 0:LON]
+
+    advance(x3b, finish, 4, pick3, None, None)
+
     add_up(rad_row, added(plane_row, in_plane, 0), in_rad, 1)
 
     packed = gram_end(0)
@@ -367,6 +402,9 @@
             vmem((3 * RAD, 24, 2 * LON), F32),
             vmem((3, 32, LON), F32),
             vmem((3, 24, LON), F32),
+            vmem((3 * RAD, 24, 2 * LON), F32),
+            vmem((3 * RAD, 24, 2 * LON), F32),
+            vmem((2, 2, pairs, RAD, LAT, LON), F32),
             vmem((3, 8, LON), F32),
             vmem((3, most - 1, 8, LON), F32),
             vmem((sizes[1] * sizes[2], LON), F32),
@@ -381,6 +419,8 @@
             dma((3,)),
             dma((2,)),
             dma((2,)),
+            pltpu.SemaphoreType.DMA,
+            pltpu.SemaphoreType.DMA,
             pltpu.SemaphoreType.REGULAR,
             pltpu.SemaphoreType.REGULAR,
         ],

time: 50.1 us -> 50.1 us (level)
  no operation moved by 1% of the time
where the time goes in v5:
time: 50.1 us; the launch traced here: 50 us
  Pallas kernels  48.7 us (97%)
  between operations  0.64 us (1%)
  other arithmetic  0.63 us (1%)
    pallas_call x1, Pallas kernels, per_device(): pl.pallas_call(functools.partial(kernel, sizes), out_shape=pltpu.VMEM((2,...  48.7 us

profile of v5, /device:TPU:1, one launch (start us, length us, event | category | flops | bytes accessed | tf_op | source)
XLA Modules:
  0.0 50.0 jit_solution(1142242827064669789)
XLA Ops:
  0.6 48.7 %filter_and_direction.1 = f32[2,4,16,128]{3,2,1,0:T(8,128)S(1)} custom-call(f32[4,16,128]{2,1,0:T(8,128)} %g_hbm.1, f32[4,16,128]{2,1,0:T(8,128)} %k_hbm.1, f32[10,4,16,128]{3,2,1,0:T(8,128)} %s_hbm.1, f32[10,4,16,128]{3,2,1,0:T(8,128)} %y_hbm.1), custom_call_target="tpu_custom_call" | custom-call | flops 20000000 | bytes 800000 | tf_op jit(solution)/shard_map/filter_and_direction/pallas_call | solution.py:384
  49.4 0.6 %negate_bitcast_fusion = (f32[4,16,128]{2,1,0:T(8,128)}, f32[4,16,128]{2,1,0:T(8,128)}) fusion(f32[2,4,16,128]{3,2,1,0:T(8,128)S(1)} %filter_and_direction.1), kind=kLoop, calls=%fused_computation | loop fusion | flops 16384 | bytes 131072 | tf_op jit(solution)/shard_map/neg | solution.py:431

commit v6 on v5

--- a/solution.py
+++ b/solution.py
@@ -54,8 +54,9 @@
     near = (0, -1, 1)
     cube = [(r, a, o) for r in near for a in near for o in near][1:]
     cube.sort(key=lambda c: -sum(map(abs, c)))
+    partners = cube + [(-2, 0, 0), (2, 0, 0)]
     barrier = pltpu.get_barrier_semaphore()
-    for offset in cube:
+    for offset in partners:
         pl.semaphore_signal(barrier, inc=1, device_id=peer(*offset), device_id_type=MESH)
 
     lane = lax.broadcasted_iota(jnp.int32, (8, LON), 1)
@@ -73,7 +74,7 @@
     edges[0] = to_left
     edges[1] = to_right
 
-    pl.semaphore_wait(barrier, len(cube))
+    pl.semaphore_wait(barrier, len(partners))
 
     own = pl.ds(RAD, RAD)
 
@@ -100,12 +101,23 @@
 
     load_s.wait()
     load_y.wait()
-    for r in (1, -1):
-        send(hist, near_hist.at[block_of(r) // 2], hist_sent, hist_here, peer(r, 0, 0))
-    owed.append((near_hist, hist_sent))
+    odd = lax.rem(me[0], 2)
+
+    def along(step):
+        return (lax.rem(me[0] + step + n_rad, n_rad), me[1], me[2])
+
+    send(hist, near_hist.at[odd], hist_sent.at[0], hist_here.at[0], along(1 - 2 * odd))
+    send(hist.at[0], near_hist.at[1 - odd, 0], hist_sent.at[1], hist_here.at[1], along(2 * odd - 1))
+    owed += [(near_hist.at[0], hist_sent.at[0]), (near_hist.at[1], hist_sent.at[1])]
+
+    def pass_on():
+        wait_bytes(near_hist.at[0], hist_here.at[0])
+        send(near_hist.at[1 - odd, 1], near_hist.at[odd, 1], hist_sent.at[1], hist_here.at[1], along(2 - 4 * odd))
 
     total = [jnp.zeros((8, LON), F32) for _ in range(-(-pairs // 4))]
     for j in range(pairs):
+        if j == pairs // 2:
+            pass_on()
         acc_s = jnp.zeros((pairs, 8, LON), F32)
         acc_y = jnp.zeros((pairs, 8, LON), F32)
         for spot in range(2 * RAD):
@@ -283,7 +295,7 @@
     spread(vb, va, 3)
     spread(va, vb, 4)
 
-    wait_bytes(near_hist, hist_here)
+    wait_bytes(near_hist.at[1], hist_here.at[1])
     acc = [jnp.zeros((pairs, 8, LON), F32) for _ in range(2)]
     for r in range(3 * RAD):
         for half in range(LAT // 8):
@@ -419,8 +431,8 @@
             dma((3,)),
             dma((2,)),
             dma((2,)),
-            pltpu.SemaphoreType.DMA,
-            pltpu.SemaphoreType.DMA,
+            dma((2,)),
+            dma((2,)),
             pltpu.SemaphoreType.REGULAR,
             pltpu.SemaphoreType.REGULAR,
         ],

time: 50.1 us -> 50.2 us (level)
  no operation moved by 1% of the time
where the time goes in v6:
time: 50.2 us; the launch traced here: 50 us
  Pallas kernels  48.7 us (97%)
  between operations  0.64 us (1%)
  other arithmetic  0.63 us (1%)
    pallas_call x1, Pallas kernels, per_device(): pl.pallas_call(functools.partial(kernel, sizes), out_shape=pltpu.VMEM((2,...  48.7 us

profile of v6, /device:TPU:1, one launch (start us, length us, event | category | flops | bytes accessed | tf_op | source)
XLA Modules:
  0.0 50.0 jit_solution(3129841179873903415)
XLA Ops:
  0.6 48.7 %filter_and_direction.1 = f32[2,4,16,128]{3,2,1,0:T(8,128)S(1)} custom-call(f32[4,16,128]{2,1,0:T(8,128)} %g_hbm.1, f32[4,16,128]{2,1,0:T(8,128)} %k_hbm.1, f32[10,4,16,128]{3,2,1,0:T(8,128)} %s_hbm.1, f32[10,4,16,128]{3,2,1,0:T(8,128)} %y_hbm.1), custom_call_target="tpu_custom_call" | custom-call | flops 20000000 | bytes 800000 | tf_op jit(solution)/shard_map/filter_and_direction/pallas_call | solution.py:396
  49.4 0.6 %negate_bitcast_fusion = (f32[4,16,128]{2,1,0:T(8,128)}, f32[4,16,128]{2,1,0:T(8,128)}) fusion(f32[2,4,16,128]{3,2,1,0:T(8,128)S(1)} %filter_and_direction.1), kind=kLoop, calls=%fused_computation | loop fusion | flops 16384 | bytes 131072 | tf_op jit(solution)/shard_map/neg | solution.py:443

commit v7 on v4

--- a/solution.py
+++ b/solution.py
@@ -41,8 +41,19 @@
         pltpu.make_async_remote_copy(src_ref=src, dst_ref=dst, send_sem=ssem, recv_sem=rsem, device_id=target,
                                      device_id_type=MESH).start()
 
+    def drain():
+        while owed:
+            wait_bytes(*owed.pop())
+
     def wait_bytes(ref, sem):
         pltpu.make_async_copy(ref, ref, sem).wait()
+
+    near = (0, -1, 1)
+    cube = [(r, a, o) for r in near for a in near for o in near][1:]
+    cube.sort(key=lambda c: -sum(map(abs, c)))
+    barrier = pltpu.get_barrier_semaphore()
+    for offset in cube:
+        pl.semaphore_signal(barrier, inc=1, device_id=peer(*offset), device_id_type=MESH)
 
     load_g = pltpu.make_async_copy(g_hbm, raw.at[0, pl.ds(RAD, RAD), pl.ds(0, LAT)], load_sem.at[0])
     load_k = pltpu.make_async_copy(k_hbm, raw.at[1, pl.ds(RAD, RAD), pl.ds(0, LAT)], load_sem.at[1])
@@ -50,13 +61,6 @@
     load_y = pltpu.make_async_copy(y_hbm, hist.at[1], load_sem.at[3])
     for copy in (load_g, load_k, load_s, load_y):
         copy.start()
-
-    near = (0, -1, 1)
-    cube = [(r, a, o) for r in near for a in near for o in near][1:]
-    cube.sort(key=lambda c: -sum(map(abs, c)))
-    barrier = pltpu.get_barrier_semaphore()
-    for offset in cube:
-        pl.semaphore_signal(barrier, inc=1, device_id=peer(*offset), device_id_type=MESH)
 
     lane = lax.broadcasted_iota(jnp.int32, (8, LON), 1)
     sub = lax.broadcasted_iota(jnp.int32, (8, LON), 0)
@@ -296,6 +300,7 @@
     in_rad = [(r, 0, 0) for r in range(1, n_rad)]
     add_up(plane_row, jnp.sum(line, axis=0, keepdims=True), in_plane, 0)
     gram_send[2, lines] = gram_end(2)
+    drain()
     gram_start(0)
     add_up(rad_row, added(plane_row, in_plane, 0), in_rad, 1)
 
@@ -326,6 +331,7 @@
     of_s = right * inverse
     of_y = -scaling * alpha
 
+    drain()
     b = added(rad_row, in_rad, 1)
     coef[0] = jnp.broadcast_to(jnp.sum(of_s * b, axis=1, keepdims=True), (16, LON))
     coef[1] = jnp.broadcast_to(jnp.sum(of_y * b, axis=1, keepdims=True), (16, LON))
@@ -336,9 +342,6 @@
             value = value + coef[0, pl.ds(i, 1)] * hist[0, i, spot // 2, rows, :]
             value = value + coef[1, pl.ds(i, 1)] * hist[1, i, spot // 2, rows, :]
         minus_dir[spot // 2, rows, :] = value
-
-    for ref, sem in owed:
-        wait_bytes(ref, sem)
 
 
 def per_device(sizes, gradient, conductance, s_hist, y_hist):

time: 50.1 us -> 50.1 us (level)
  no operation moved by 1% of the time
where the time goes in v7:
time: 50.1 us; the launch traced here: 49.9 us
  Pallas kernels  48.6 us (97%)
  between operations  0.64 us (1%)
  other arithmetic  0.63 us (1%)
    pallas_call x1, Pallas kernels, per_device(): pl.pallas_call(functools.partial(kernel, sizes), out_shape=pltpu.VMEM((2,...  48.6 us

profile of v7, /device:TPU:1, one launch (start us, length us, event | category | flops | bytes accessed | tf_op | source)
XLA Modules:
  0.0 49.9 jit_solution(15100876561405692367)
XLA Ops:
  0.6 48.6 %filter_and_direction.1 = f32[2,4,16,128]{3,2,1,0:T(8,128)S(1)} custom-call(f32[4,16,128]{2,1,0:T(8,128)} %g_hbm.1, f32[4,16,128]{2,1,0:T(8,128)} %k_hbm.1, f32[10,4,16,128]{3,2,1,0:T(8,128)} %s_hbm.1, f32[10,4,16,128]{3,2,1,0:T(8,128)} %y_hbm.1), custom_call_target="tpu_custom_call" | custom-call | flops 20000000 | bytes 800000 | tf_op jit(solution)/shard_map/filter_and_direction/pallas_call | solution.py:352
  49.3 0.6 %negate_bitcast_fusion = (f32[4,16,128]{2,1,0:T(8,128)}, f32[4,16,128]{2,1,0:T(8,128)}) fusion(f32[2,4,16,128]{3,2,1,0:T(8,128)S(1)} %filter_and_direction.1), kind=kLoop, calls=%fused_computation | loop fusion | flops 16384 | bytes 131072 | tf_op jit(solution)/shard_map/neg | solution.py:394

commit v8 on v6

--- a/solution.py
+++ b/solution.py
@@ -54,7 +54,7 @@
     near = (0, -1, 1)
     cube = [(r, a, o) for r in near for a in near for o in near][1:]
     cube.sort(key=lambda c: -sum(map(abs, c)))
-    partners = cube + [(-2, 0, 0), (2, 0, 0)]
+    partners = cube + [(-2, 0, 0), (2, 0, 0)] + [(0, a, 0) for a in range(2, n_lat - 1)]
     barrier = pltpu.get_barrier_semaphore()
     for offset in partners:
         pl.semaphore_signal(barrier, inc=1, device_id=peer(*offset), device_id_type=MESH)
@@ -134,14 +134,6 @@
         gram_send[0, pl.ds(line, 1)] = jnp.sum(value, axis=0, keepdims=True)
     lines = pl.ds(0, len(total))
 
-    for ref, number in halos:
-        wait_bytes(ref, halo_here.at[number])
-
-    signs = (0, -2, 2)
-    outer = [(0, a, o) for a in signs for o in signs][1:] + [(-2, 0, 0), (2, 0, 0)]
-    for offset in outer:
-        pl.semaphore_signal(near_in, inc=1, device_id=peer(*offset), device_id_type=MESH)
-
     turn = {1: 0, 2: 1, 0: 2}
 
     def gram_start(stage):
@@ -157,6 +149,16 @@
         ref = gram_recv.at[at, pl.ds(0, sizes[stage] - 1), lines]
         wait_bytes(ref, gram_here.at[at])
         return gram_send[at, lines] + jnp.sum(gram_recv[at, pl.ds(0, sizes[stage] - 1), lines], axis=0)
+
+    gram_start(1)
+
+    for ref, number in halos:
+        wait_bytes(ref, halo_here.at[number])
+
+    signs = (0, -2, 2)
+    outer = [(0, a, o) for a in signs for o in signs][1:] + [(-2, 0, 0), (2, 0, 0)]
+    for offset in outer:
+        pl.semaphore_signal(near_in, inc=1, device_id=peer(*offset), device_id_type=MESH)
 
     low_rad = (me[0] > 0).astype(F32)
     high_rad = (me[0] < n_rad - 1).astype(F32)
@@ -262,15 +264,14 @@
     pl.semaphore_wait(near_in, len(outer))
     for r in (-4, 4):
         pl.semaphore_signal(far_in, inc=1, device_id=peer(r, 0, 0), device_id_type=MESH)
-    gram_start(1)
+    gram_send[1, lines] = gram_end(1)
+    gram_start(2)
     exchanged(x2a, side2, 0)
     advance(x2a, store(x2b), 1, pick2, low_rad, high_rad, side2)
     advance(x2b, store(x2c), 2, pick2, None, None)
     advance(x2c, store(x2b), 3, pick2, None, None)
     advance(x2b, keep3, 4, pick2, None, None)
     exchange(x3a, side3, 1)
-    gram_send[1, lines] = gram_end(1)
-    gram_start(2)
 
     def spread(src, dst, step):
         first, last = RAD - step, 2 * RAD - 1 + step

time: 50.2 us -> 48.4 us (0.964)
  Pallas kernels: 48.7 us -> 47 us
    pallas_call x1, Pallas kernels: 48.7 us -> 47 us  [per_device(): pl.pallas_call(functools.partial(kernel, sizes), out_shape=pltpu.VMEM((2,...]
where the time goes in v8:
time: 48.4 us; the launch traced here: 48.2 us
  Pallas kernels  47 us (97%)
  between operations  0.64 us (1%)
  other arithmetic  0.63 us (1%)
    pallas_call x1, Pallas kernels, per_device(): pl.pallas_call(functools.partial(kernel, sizes), out_shape=pltpu.VMEM((2,...  47 us

profile of v8, /device:TPU:1, one launch (start us, length us, event | category | flops | bytes accessed | tf_op | source)
XLA Modules:
  0.0 48.2 jit_solution(13940472688640901611)
XLA Ops:
  0.6 47.0 %filter_and_direction.1 = f32[2,4,16,128]{3,2,1,0:T(8,128)S(1)} custom-call(f32[4,16,128]{2,1,0:T(8,128)} %g_hbm.1, f32[4,16,128]{2,1,0:T(8,128)} %k_hbm.1, f32[10,4,16,128]{3,2,1,0:T(8,128)} %s_hbm.1, f32[10,4,16,128]{3,2,1,0:T(8,128)} %y_hbm.1), custom_call_target="tpu_custom_call" | custom-call | flops 20000000 | bytes 800000 | tf_op jit(solution)/shard_map/filter_and_direction/pallas_call | solution.py:397
  47.6 0.6 %negate_bitcast_fusion = (f32[4,16,128]{2,1,0:T(8,128)}, f32[4,16,128]{2,1,0:T(8,128)}) fusion(f32[2,4,16,128]{3,2,1,0:T(8,128)S(1)} %filter_and_direction.1), kind=kLoop, calls=%fused_computation | loop fusion | flops 16384 | bytes 131072 | tf_op jit(solution)/shard_map/neg | solution.py:444
